TPU v7x, 32 devices: a whole 2x2x4 slice. The times are simulated.
32 devices in a mesh: ping: 8 (over y, x, core), rng: 4 (over z).
Axes of the slice: x: 2, y: 2, z: 4, core: 2. Of those that a mesh axis runs over, the one named last changes fastest.
Arguments:
- echoes: bfloat16 [128, 2, 32, 8192], P('ping', None, None, 'rng'), may hold values from -36 to 36, as said below
- pairing: int32 [128, 2, 8], P('ping'), may hold values from 0 to 31, as said below
- footprint: int32 [8, 48], replicated, may hold values from 0 to 127, as said below
- counts: int32 [8], replicated, may hold values from 1 to 48, 128 in all
- offsets: int32 [8, 48], replicated, may hold values from -64 to 64
- earlier: bfloat16 [8, 2, 1024, 8192], P('ping', None, None, 'rng'), may hold values from -6 to 6
Outputs:
- image: bfloat16 [8, 2, 1024, 8192], P('ping', None, None, 'rng')
Inputs may be any that keep to these rules, and one draw needn't show every extreme that they name: `echoes`: the samples of a ping's pairing[p, 1] channels are partly a turned copy of ping p - 1's pairing[p, 0] channels. `pairing`: for each ping the 16 channels of its two rows are all different. `footprint`: the first counts[t] entries of row t are the pings that see tile t; the 48 entries of a row are different pings, and no aligned block of 16 pings (the pings of one ping owner, starting at a multiple of 16) holds more than 6 of them. `counts`: they sum to 128.
All inputs are finite; a program needn't handle non-finite values.
Results may differ from a plain program's by a relative error of at most 0.0053.
Values may be sent and summed in bfloat16 or wider, within the bound.
No kernel may reach another device: no remote copies, remote signals or barrier semaphores. Data moves between devices by JAX's collectives and lax.ppermute only.
A program may use at most 192 MiB of HBM per device.

v0:
```python
import math

import jax
import jax.numpy as jnp
from jax import lax
from jax.sharding import PartitionSpec as P

C = 32
X = 1024
BAND = 64
MOST = 48
TILE_DEV = 1
PING_DEV = 16


phase_modulus = 4099
small_value = 1e-06


def passed_along(shard, axis, by):
    length = lax.axis_size(axis)
    pairs = [(i, i + by) for i in range(length) if 0 <= i + by < length]
    return lax.ppermute(shard, axis, pairs)


def prefix(shard, axis, combine, identity):
    length, position = (lax.axis_size(axis), lax.axis_index(axis))
    everything = lax.all_gather(shard, axis)
    start = jnp.broadcast_to(jnp.asarray(identity, shard.dtype), shard.shape)

    def step(k, before):
        reached = k < position
        new = combine(before, everything[k])
        return jnp.where(reached, new, before)

    return lax.fori_loop(0, length, step, start)


def with_halo(cells, sides, width):
    for axis, dim in sides:
        count = lax.axis_size(axis)
        ends = count - 1
        head = lax.slice_in_dim(cells, 0, width, axis=dim)
        tail = lax.slice_in_dim(cells, cells.shape[dim] - width, cells.shape[dim], axis=dim)
        cells = jnp.concatenate(
            [
                lax.ppermute(tail, axis, [(i, (i + 1) % count) for i in range(ends)]),
                cells,
                lax.ppermute(head, axis, [((i + 1) % count, i) for i in range(ends)]),
            ],
            axis=dim,
        )
    return cells


def weight_matrix(tile_id, ping_ids, shift_ids, live_rows, tile_count):
    spacing = TILE_DEV * X // PING_DEV
    column = jnp.arange(ping_ids.shape[0] * 2 * C, dtype=jnp.int32)
    part_of = column // C % 2
    channel = column % C
    ping_cols = jnp.repeat(ping_ids, 2 * C)
    shift_cols = jnp.repeat(shift_ids, 2 * C)
    live_cols = jnp.repeat(live_rows, 2 * C)
    pixels = jnp.arange(X, dtype=jnp.int32)
    offset = tile_id * X - ping_cols * spacing - 2 * channel
    folded = jnp.remainder(pixels[:, None] + offset[None, :], phase_modulus)
    square = jnp.remainder(folded * folded, phase_modulus)
    phases = square.astype(jnp.float32) * (2.0 * math.pi / phase_modulus) + shift_cols.astype(
        jnp.float32
    )[None, :] * (math.pi / 4.0)
    scales = live_cols / jnp.sqrt(jnp.float32(C) * tile_count.astype(jnp.float32))
    cosine = jnp.cos(phases) * scales[None, :]
    sines = jnp.sin(phases) * scales[None, :]
    upper_rows = jnp.where(part_of[None, :] == 0, cosine, -sines)
    lower_rows = jnp.where(part_of[None, :] == 0, sines, cosine)
    return jnp.concatenate([upper_rows, lower_rows], axis=0).astype(jnp.bfloat16)


def focus_tile(received_data, received_labels):
    flat_rows = received_data.reshape((-1,) + received_data.shape[2:])
    flat_labels = received_labels.reshape(-1, 4)
    live_int = (flat_labels[:, 0] >= 0).astype(jnp.int32)
    ping_ids = flat_labels[:, 1]
    shift_ids = flat_labels[:, 2]
    tile_id = flat_labels[0, 3]
    tile_count = jnp.sum(live_int)
    block_len = flat_rows.shape[3]
    weights = weight_matrix(tile_id, ping_ids, shift_ids, live_int.astype(jnp.float32), tile_count)
    product = jnp.dot(weights, flat_rows.reshape(-1, block_len), preferred_element_type=jnp.float32)
    return product.reshape(2, X, block_len)


def focus(received):
    received_data, received_labels = received
    results = [focus_tile(received_data[:, 0], received_labels[:, 0])]
    return jnp.stack(results, axis=0)


def per_device(echoes, pairing, footprint, counts, offsets, earlier):
    ping_dev = echoes.shape[0]
    owners = lax.axis_size("ping")
    own_index = lax.axis_index("ping")
    channel_ids = jnp.arange(C, dtype=jnp.int32)
    front_pick = (pairing[:, 0, :, None] == channel_ids).astype(jnp.bfloat16)
    rear_pick = (pairing[:, 1, :, None] == channel_ids).astype(jnp.bfloat16)
    rear_rows = jnp.einsum("pkc,pzcr->pzkr", rear_pick, echoes, preferred_element_type=jnp.float32)
    inner_rows = jnp.einsum(
        "pkc,pzcr->pzkr", front_pick[1:], echoes[:-1], preferred_element_type=jnp.float32
    )
    last_ping = passed_along(echoes[-1], "ping", 1)
    lead_rows = jnp.einsum(
        "kc,zcr->zkr", front_pick[0], last_ping, preferred_element_type=jnp.float32
    )
    front_rows = jnp.concatenate([lead_rows[None], inner_rows], axis=0)
    cross_sum = jnp.sum(
        front_rows[:, 0] * rear_rows[:, 1] - front_rows[:, 1] * rear_rows[:, 0], axis=(1, 2)
    )
    front_energy = jnp.sum(front_rows * front_rows, axis=(1, 2, 3))
    rear_energy = jnp.sum(rear_rows * rear_rows, axis=(1, 2, 3))
    cross_sum, front_energy, rear_energy = lax.psum((cross_sum, front_energy, rear_energy), "rng")
    increment = cross_sum / (jnp.sqrt(front_energy * rear_energy) + small_value)
    running = jnp.cumsum(increment)
    before_turn = prefix(running[-1], "ping", jnp.add, jnp.float32(0.0))
    track_turn = before_turn + running
    cosine = jnp.cos(track_turn)[:, None, None]
    sines = jnp.sin(track_turn)[:, None, None]
    real_part = echoes[:, 0].astype(jnp.float32)
    imag_part = echoes[:, 1].astype(jnp.float32)
    corrected = jnp.stack(
        [real_part * cosine + imag_part * sines, imag_part * cosine - real_part * sines], axis=1
    ).astype(jnp.bfloat16)
    tile_total = footprint.shape[0]
    slot_cap = -(-MOST // owners)
    positions = jnp.arange(MOST, dtype=jnp.int32)
    in_list = positions[None, :] < counts[:, None]
    from_here = in_list & (footprint // ping_dev == own_index)
    order_here = jnp.cumsum(from_here.astype(jnp.int32), axis=1) - 1
    slot_ids = jnp.arange(slot_cap, dtype=jnp.int32)
    select = (from_here[:, None, :] & (order_here[:, None, :] == slot_ids[None, :, None])).astype(
        jnp.int32
    )
    place_ids = jnp.sum(select * (positions + 1)[None, None, :], axis=2) - 1
    local_ids = jnp.sum(select * (footprint % ping_dev)[:, None, :], axis=2)
    ping_ids = jnp.sum(select * footprint[:, None, :], axis=2)
    shift_ids = jnp.sum(select * offsets[:, None, :], axis=2)
    tile_ids = jnp.broadcast_to(jnp.arange(tile_total, dtype=jnp.int32)[:, None], place_ids.shape)
    labels = jnp.stack([place_ids, ping_ids, shift_ids, tile_ids], axis=2).reshape(
        owners, tile_total // owners, slot_cap, 4
    )
    block_len = corrected.shape[3]
    source = with_halo(corrected, (("rng", 3),), BAND)

    def cut_window(local_one, offset_one):
        return lax.dynamic_slice(
            source, (local_one, 0, 0, BAND + offset_one), (1, 2, C, block_len)
        )[0]

    outgoing = jax.vmap(cut_window)(local_ids.reshape(-1), shift_ids.reshape(-1))
    outgoing = outgoing.reshape((owners, tile_total // owners, slot_cap, 2, C, block_len))
    contribution = focus(
        (
            lax.all_to_all(outgoing, "ping", split_axis=0, concat_axis=0, tiled=True),
            lax.all_to_all(labels, "ping", split_axis=0, concat_axis=0, tiled=True),
        )
    )
    return (earlier.astype(jnp.float32) + contribution).astype(jnp.bfloat16)


def solution(mesh):
    return jax.shard_map(
        per_device,
        mesh=mesh,
        in_specs=(
            P("ping", None, None, "rng"),
            P("ping", None, None),
            P(),
            P(),
            P(),
            P("ping", None, None, "rng"),
        ),
        out_specs=P("ping", None, None, "rng"),
        check_vma=False,
    )
```

profile of v0, /device:TPU:0, one launch (start us, length us, event | category | flops | bytes accessed | tf_op | source)
XLA Modules:
  0.0 442.8 jit_solution(9715342319560469879)
XLA Ops:
  7.1 5.0 %all-to-all-start = ((s32[8,1,6,4]{2,3,1,0:T(4,128)}), s32[8,1,6,4]{2,3,1,0:T(4,128)S(1)}, u32[]{:S(2)}, u32[]{:S(2)}) async-start(s32[8,1,6,4]{2,3,1,0:T(4,128)} %copy.21), calls=%async_computation | async-start | bytes 32768 | tf_op jit(solution)/shard_map/all_to_all | solution.py:163
  15.8 4.2 multiply_reduce_fusion
  23.6 12.0 %all-reduce.1 = (f32[16]{0:T(128)S(1)}, f32[16]{0:T(128)S(1)}, f32[16]{0:T(128)S(1)}) all-reduce(f32[16]{0:T(128)S(1)} %fusion.26, f32[16]{0:T(128)S(1)} %fusion.22, f32[16]{0:T(128)S(1)} %get-tuple-element.136), channel_id=1, replica_groups=mesh['ping'=8,'rng'=4] {'rng'}, use_global_device_ids=true, to_apply=%region_6.0 | all-reduce | flops 48 | bytes 384 | tf_op jit(solution)/shard_map/psum | solution.py:120
  37.6 12.4 %all-reduce = f32[8]{0:T(128)S(1)} all-reduce(f32[8]{0:T(128)S(1)} %bitcast_dynamic-update-slice_fusion.1), channel_id=2, replica_groups=mesh['ping'=8,'rng'=4] {'ping'}, use_global_device_ids=true, to_apply=%add | all-reduce | flops 8 | bytes 64 | tf_op jit(solution)/shard_map/all_gather | solution.py:28
  50.1 10.0 %while.14 = (s32[]{:T(128)}, f32[]{:T(128)}, s32[]{:T(128)}, f32[8]{0:T(128)S(1)}, s32[]{:T(128)}) while((s32[]{:T(128)}, f32[]{:T(128)}, s32[]{:T(128)}, f32[8]{0:T(128)S(1)}, s32[]{:T(128)}) %tuple.56), condition=%wide.region_13.14_spmd, body=%wide.region_12.13_spmd.sunk | while | flops 5 | bytes 107 | solution.py:36
  60.3 3.8 fusion.15
  71.2 4.1 collective-permute-done.2
  75.3 9.0 %concatenate.18 = bf16[16,2,32,2176]{3,2,1,0:T(8,128)(2,1)} concatenate(bf16[16,2,32,64]{3,2,1,0:T(8,128)(2,1)S(1)} %collective-permute-done.1, bf16[16,2,32,2048]{3,2,1,0:T(8,128)(2,1)} %pad_maximum_fusion.1, bf16[16,2,32,64]{3,2,1,0:T(8,128)(2,1)S(1)} %collective-permute-done.2), dimensions={3} | concatenate | bytes 8912896 | tf_op jit(solution)/shard_map/concatenate | solution.py:45
  84.3 179.6 %while.15 = (s32[]{:T(128)}, bf16[16,2,32,2176]{3,2,1,0:T(8,128)(2,1)}, s32[48,4]{0,1:T(4,128)S(1)}, bf16[48,1,2,32,2048]{4,3,2,1,0:T(8,128)(2,1)}, s32[]{:T(128)}) while((s32[]{:T(128)}, bf16[16,2,32,2176]{3,2,1,0:T(8,128)(2,1)}, s32[48,4]{0,1:T(4,128)S(1)}, bf16[48,1,2,32,2048]{4,3,2,1,0:T(8,128)(2,1)}, s32[]{:T(128)}) %tuple.59), condition=%wide.while_cond, body=%wide.while_body.sunk | while | flops 2 | bytes 525937 | solution.py:154
  96.2 3.1 bitcast_dynamic-update-slice_fusion.3
  99.9 3.1 bitcast_dynamic-update-slice_fusion.3
  103.7 3.1 bitcast_dynamic-update-slice_fusion.3
  107.4 3.1 bitcast_dynamic-update-slice_fusion.3
  111.2 3.1 bitcast_dynamic-update-slice_fusion.3
  114.9 3.1 bitcast_dynamic-update-slice_fusion.3
  126.1 3.1 bitcast_dynamic-update-slice_fusion.3
  129.9 3.1 bitcast_dynamic-update-slice_fusion.3
  133.7 3.1 bitcast_dynamic-update-slice_fusion.3
  141.1 3.1 bitcast_dynamic-update-slice_fusion.3
  152.3 3.1 bitcast_dynamic-update-slice_fusion.3
  156.1 3.1 bitcast_dynamic-update-slice_fusion.3
  159.8 3.1 bitcast_dynamic-update-slice_fusion.3
  163.6 3.1 bitcast_dynamic-update-slice_fusion.3
  167.3 3.1 bitcast_dynamic-update-slice_fusion.3
  171.1 3.1 bitcast_dynamic-update-slice_fusion.3
  174.8 3.1 bitcast_dynamic-update-slice_fusion.3
  178.5 3.1 bitcast_dynamic-update-slice_fusion.3
  182.3 3.1 bitcast_dynamic-update-slice_fusion.3
  186.0 3.1 bitcast_dynamic-update-slice_fusion.3
  189.8 3.1 bitcast_dynamic-update-slice_fusion.3
  201.0 3.1 bitcast_dynamic-update-slice_fusion.3
  204.7 3.1 bitcast_dynamic-update-slice_fusion.3
  208.5 3.1 bitcast_dynamic-update-slice_fusion.3
  212.2 3.1 bitcast_dynamic-update-slice_fusion.3
  216.0 3.1 bitcast_dynamic-update-slice_fusion.3
  219.7 3.1 bitcast_dynamic-update-slice_fusion.3
  223.5 3.1 bitcast_dynamic-update-slice_fusion.3
  227.2 3.1 bitcast_dynamic-update-slice_fusion.3
  231.0 3.1 bitcast_dynamic-update-slice_fusion.3
  234.7 3.1 bitcast_dynamic-update-slice_fusion.3
  238.5 3.1 bitcast_dynamic-update-slice_fusion.3
  242.2 3.1 bitcast_dynamic-update-slice_fusion.3
  260.9 3.1 bitcast_dynamic-update-slice_fusion.3
  264.0 5.6 %all-to-all-start.1 = ((bf16[8,1,6,2,32,2048]{5,4,3,2,1,0:T(8,128)(2,1)}), bf16[8,1,6,2,32,2048]{5,4,3,2,1,0:T(8,128)(2,1)}, u32[]{:S(2)}, u32[]{:S(2)}) async-start(bf16[8,1,6,2,32,2048]{5,4,3,2,1,0:T(8,128)(2,1)} %bitcast.77), calls=%async_computation.1 | async-start | bytes 25165824 | tf_op jit(solution)/shard_map/all_to_all | solution.py:162
  272.6 61.1 %select_convert_fusion.1 = (bf16[1024,3072]{1,0:T(8,128)(2,1)S(1)}, bf16[1024,3072]{1,0:T(8,128)(2,1)S(1)}) fusion(f32[3072]{0:T(1024)S(1)} %div.51, f32[3072]{0:T(1024)S(1)} %mul.166, s32[3072]{0:T(1024)S(1)} %fusion.44, pred[3072]{0:T(1024)(128)(4,1)S(1)} %fusion.42), kind=kLoop, calls=%fused_computation.13 | loop fusion | flops 75497472 | bytes 12622848 | tf_op jit(solution)/shard_map/convert.2
  333.7 5.6 %pad_maximum_fusion = bf16[2048,3072]{1,0:T(8,128)(2,1)} fusion(bf16[1024,3072]{1,0:T(8,128)(2,1)S(1)} %get-tuple-element.127, bf16[1024,3072]{1,0:T(8,128)(2,1)S(1)} %get-tuple-element.126), kind=kLoop, calls=%fused_computation.11 | loop fusion | flops 25165824 | bytes 25165824 | tf_op jit(solution)/shard_map/concatenate | solution.py:76
  339.4 69.0 %all-to-all-done.1 = bf16[8,1,6,2,32,2048]{5,4,3,2,1,0:T(8,128)(2,1)} async-done(((bf16[8,1,6,2,32,2048]{5,4,3,2,1,0:T(8,128)(2,1)}), bf16[8,1,6,2,32,2048]{5,4,3,2,1,0:T(8,128)(2,1)}, u32[]{:S(2)}, u32[]{:S(2)}) %all-to-all-start.1) | async-done | bytes 12582944 | tf_op jit(solution)/shard_map/all_to_all | solution.py:162
  408.4 34.4 %fusion = bf16[1,2,1024,2048]{3,2,1,0:T(8,128)(2,1)} fusion(bf16[1,2,1024,2048]{3,2,1,0:T(8,128)(2,1)} %param.13, bf16[2,1024,3072]{2,1,0:T(8,128)(2,1)} %bitcast.78, bf16[3072,2048,1]{1,0,2:T(8,128)(2,1)} %bitcast.28), kind=kOutput, calls=%fused_computation.5 | convolution fusion | flops 25782386688 | bytes 41943040 | tf_op jit(solution)/shard_map/dot_general | solution.py:89
  (183 shorter events, 104.3 us)
Async XLA Ops:
  1.0 20.4 %collective-permute-start = (bf16[2,32,2048]{2,1,0:T(8,128)(2,1)S(1)}, bf16[2,32,2048]{2,1,0:T(8,128)(2,1)S(1)}, u32[]{:S(2)}, u32[]{:S(2)}) collective-permute-start(bf16[2,32,2048]{2,1,0:T(8,128)(2,1)S(1)} %slice_bitcast_fusion), channel_id=1, source_target_pairs={{0,4},{4,8},{8,12},{12,16},{16,20},{20,24},{24,28},{1,5},{5,9},{9,... | collective-permute-start | bytes 786440 | tf_op jit(solution)/shard_map/ppermute | solution.py:23
  7.1 256.9 %all-to-all-start = ((s32[8,1,6,4]{2,3,1,0:T(4,128)}), s32[8,1,6,4]{2,3,1,0:T(4,128)S(1)}, u32[]{:S(2)}, u32[]{:S(2)}) async-start(s32[8,1,6,4]{2,3,1,0:T(4,128)} %copy.21), calls=%async_computation | async-start | bytes 32768 | tf_op jit(solution)/shard_map/all_to_all | solution.py:163
  15.7 4.9 %copy-start = (u32[32]{0:T(128)S(1)}, u32[32]{0:T(128)}, u32[]{:S(2)}) copy-start(u32[32]{0:T(128)} %constant.165) | copy-start | bytes 388
  64.3 6.9 %collective-permute-start.1 = (bf16[16,2,32,64]{3,2,1,0:T(8,128)(2,1)S(1)}, bf16[16,2,32,64]{3,2,1,0:T(8,128)(2,1)S(1)}, u32[]{:S(2)}, u32[]{:S(2)}) collective-permute-start(bf16[16,2,32,64]{3,2,1,0:T(8,128)(2,1)S(1)} %get-tuple-element.125), channel_id=1, source_target_pairs={{0,1},{1,2},{2,3},{4,5},{5,6},{6,7},{8,9},{9,10},{10,11},{12,13},{... | collective-permute-start | bytes 393224 | tf_op jit(solution)/shard_map/ppermute | solution.py:47
  65.6 9.7 %collective-permute-start.2 = (bf16[16,2,32,64]{3,2,1,0:T(8,128)(2,1)S(1)}, bf16[16,2,32,64]{3,2,1,0:T(8,128)(2,1)S(1)}, u32[]{:S(2)}, u32[]{:S(2)}) collective-permute-start(bf16[16,2,32,64]{3,2,1,0:T(8,128)(2,1)S(1)} %get-tuple-element.124), channel_id=1, source_target_pairs={{1,0},{2,1},{3,2},{5,4},{6,5},{7,6},{9,8},{10,9},{11,10},{13,12},{... | collective-permute-start | bytes 393224 | tf_op jit(solution)/shard_map/ppermute | solution.py:49
  264.0 144.4 %all-to-all-start.1 = ((bf16[8,1,6,2,32,2048]{5,4,3,2,1,0:T(8,128)(2,1)}), bf16[8,1,6,2,32,2048]{5,4,3,2,1,0:T(8,128)(2,1)}, u32[]{:S(2)}, u32[]{:S(2)}) async-start(bf16[8,1,6,2,32,2048]{5,4,3,2,1,0:T(8,128)(2,1)} %bitcast.77), calls=%async_computation.1 | async-start | bytes 25165824 | tf_op jit(solution)/shard_map/all_to_all | solution.py:162
where the time goes:
time: 450 us; the launch traced here: 443 us
  local copies, waits for them, and re-layouts  200 us (44%)
  other arithmetic  79.1 us (18%)
  waiting for transfers between devices  75.1 us (17%)
  matrix products  41.5 us (9%)
  blocking collectives  24.4 us (5%)
  starting transfers between devices  15.5 us (3%)
  loops' own time  5.43 us (1%)
    gather x144, local copies, waits for them, and re-layouts  180 us
    all_to_all x1, waiting for transfers between devices, per_device(): lax.all_to_all(outgoing, 'ping', split_axis=0, concat_axis=0, tiled=True)  69 us
    another operation x3, other arithmetic  65 us
    dot_general x1, matrix products, focus_tile(): jnp.dot(weights, flat_rows.reshape(-1, block_len), preferred_element_type...  34.4 us
    all_gather x1, blocking collectives, prefix(): everything = lax.all_gather(shard, axis)  12.4 us
    psum x1, blocking collectives, per_device(): lax.psum((cross_sum, front_energy, rear_energy), 'rng')  12 us
    concatenate x1, local copies, waits for them, and re-layouts, with_halo(): jnp.concatenate([lax.ppermute(tail, axis, [(i, (i + 1) % count) for i in...  9.04 us
  transfers between devices with their start and end apart: 5, of which 3 were waited for; matrix products, arithmetic and copies ran while one was open for 64% of the time, Pallas kernels for 0%

commit v1 on v0

--- a/solution.py
+++ b/solution.py
@@ -1,8 +1,12 @@
+import functools
 import math
 
 import jax
 import jax.numpy as jnp
+import numpy as np
 from jax import lax
+from jax.experimental import pallas as pl
+from jax.experimental.pallas import tpu as pltpu
 from jax.sharding import PartitionSpec as P
 
 C = 32
@@ -96,7 +100,7 @@
     return jnp.stack(results, axis=0)
 
 
-def per_device(echoes, pairing, footprint, counts, offsets, earlier):
+def general_device(echoes, pairing, footprint, counts, offsets, earlier):
     ping_dev = echoes.shape[0]
     owners = lax.axis_size("ping")
     own_index = lax.axis_index("ping")
@@ -166,6 +170,550 @@
     return (earlier.astype(jnp.float32) + contribution).astype(jnp.bfloat16)
 
 
+LEAD = 4
+VARIANTS = ((4, 4, 4), (4, 4, 4, 2), (4, 4, 4, 4, 4, 4))
+LANES = 128
+MIB = 1 << 20
+SMEM = pl.BlockSpec(memory_space=pltpu.SMEM)
+ANY = pl.BlockSpec(memory_space=pl.ANY)
+COS_TERMS = (
+    1.0, -19.73920440673828, 64.93911743164062, -85.45014190673828, 60.16762924194336,
+    -25.967599868774414, 6.528658390045166,
+)
+SIN_TERMS = (
+    6.2831854820251465, -41.34170150756836, 81.60513305664062, -76.70301818847656, 42.02592849731445,
+    -14.899847030639648, 3.2381374835968018,
+)
+
+
+def bit_count(mask):
+    mask = mask - ((mask >> 1) & 0x5555)
+    mask = (mask & 0x3333) + ((mask >> 2) & 0x3333)
+    mask = (mask + (mask >> 4)) & 0x0F0F
+    return (mask + (mask >> 8)) & 0x1F
+
+
+def each_bit(mask, place, visit):
+    def body(_, carry):
+        left, at = carry
+        low = left & -left
+        visit(at, bit_count(low - 1))
+        return left ^ low, at + 1
+
+    return lax.fori_loop(0, bit_count(mask), body, (mask, place))[1]
+
+
+def link_list(masks, owners, s, axis, own, relay):
+    chips = owners // 2
+    near, other = (1, 4) if axis == 0 else (2, 2)
+    base = owners * chips
+    first = masks[base + axis * owners + s]
+    direct = masks[s * chips + ((s >> 1) ^ near)] & ~first
+    behind = s ^ other
+    passed = masks[base + (1 - axis) * owners + behind]
+    place = each_bit(first, jnp.int32(0), own)
+    place = each_bit(direct, place, own)
+    begin = jnp.maximum(place, 2 * LEAD)
+    each_bit(passed, begin, lambda at, bit: relay(at, behind, bit, at - begin))
+
+
+def plan_kernel(owners, ping_dev, cap, most, tiles, fp, cnt, me_ref, send, masks, total):
+    chips = owners // 2
+    shift = ping_dev.bit_length() - 1
+    room = 4 * cap
+    base = owners * chips
+    me = me_ref[0]
+
+    def clear(i, _):
+        masks[i] = 0
+        return 0
+
+    lax.fori_loop(0, base, clear, 0)
+
+    def clear_send(i, _):
+        send[i] = 0
+        return 0
+
+    lax.fori_loop(0, 2 * room + 2 * cap, clear_send, 0)
+
+    def one_tile(t, _):
+        def entry(j, _):
+            p = fp[t, j]
+            at = (p >> shift) * chips + (t >> 1)
+            masks[at] = masks[at] | lax.shift_left(jnp.int32(1), p & (ping_dev - 1))
+            return 0
+
+        return lax.fori_loop(0, cnt[t], entry, 0)
+
+    lax.fori_loop(0, tiles, one_tile, 0)
+
+    def split(s, _):
+        chip = s >> 1
+        far = masks[s * chips + (chip ^ 3)]
+        n = bit_count(far)
+        over_y = bit_count(masks[(s ^ 2) * chips + (chip ^ 3)])
+        over_x = bit_count(masks[(s ^ 4) * chips + (chip ^ 3)])
+        want = (n + over_x - over_y + 1) >> 1
+        want = jnp.minimum(jnp.maximum(want, jnp.maximum(n - cap, 0)), jnp.minimum(n, cap))
+
+        def take(_, carry):
+            left, taken = carry
+            low = left & -left
+            return left ^ low, taken | low
+
+        left, taken = lax.fori_loop(0, want, take, (far, jnp.int32(0)))
+        masks[base + s] = taken
+        masks[base + owners + s] = left
+        return 0
+
+    lax.fori_loop(0, owners, split, 0)
+
+    def longest(s, most_yet):
+        for axis, near, other in ((0, 1, 4), (1, 2, 2)):
+            own = bit_count(masks[base + axis * owners + s] | masks[s * chips + ((s >> 1) ^ near)])
+            passed = bit_count(masks[base + (1 - axis) * owners + (s ^ other)])
+            length = jnp.where(passed > 0, jnp.maximum(own, 2 * LEAD) + passed, own)
+            most_yet = jnp.maximum(most_yet, length)
+        return most_yet
+
+    total[0] = lax.fori_loop(0, owners, longest, jnp.int32(0))
+
+    for axis in range(2):
+
+        def own(at, bit, axis=axis):
+            send[axis * room + at] = bit
+
+        def relay(at, behind, bit, i, axis=axis):
+            send[axis * room + at] = ping_dev + i
+
+        link_list(masks, owners, me, axis, own, relay)
+
+    for k, tile in ((0, me), (1, me ^ 1)):
+
+        def mine(j, at, k=k, tile=tile):
+            p = fp[tile, j]
+            here = (p >> shift) == me
+
+            @pl.when(here)
+            def _():
+                send[2 * room + k * cap + at] = p & (ping_dev - 1)
+
+            return at + here.astype(jnp.int32)
+
+        lax.fori_loop(0, cnt[tile], mine, jnp.int32(0))
+
+
+def places_kernel(owners, ping_dev, cap, fp, cnt, off, masks, me_ref, table, back):
+    shift = ping_dev.bit_length() - 1
+    room = 4 * cap
+    count = 4 * room + 2 * cap
+    me = me_ref[0]
+
+    def clear(i, _):
+        table[i] = 0
+        return 0
+
+    lax.fori_loop(0, 3 * count, clear, 0)
+
+    def clear_back(i, _):
+        back[i] = 0
+        return 0
+
+    lax.fori_loop(0, owners * ping_dev, clear_back, 0)
+
+    def note(j, _):
+        back[fp[me, j]] = j + 1
+        return 0
+
+    lax.fori_loop(0, cnt[me], note, 0)
+
+    def put(at, ping):
+        j = back[ping]
+        table[at] = ping
+        table[count + at] = off[me, jnp.maximum(j - 1, 0)]
+        table[2 * count + at] = (j > 0).astype(jnp.int32)
+
+    for a, (axis, flip) in enumerate(((0, 2), (1, 4), (0, 3), (1, 5))):
+        s = me ^ flip
+
+        def own(at, bit, a=a, s=s):
+            put(a * room + at, s * ping_dev + bit)
+
+        def relay(at, behind, bit, i, a=a):
+            put(a * room + at, behind * ping_dev + bit)
+
+        link_list(masks, owners, s, axis, own, relay)
+
+    for k, s in ((0, me), (1, me ^ 1)):
+
+        def listed(j, at, k=k, s=s):
+            p = fp[me, j]
+            here = (p >> shift) == s
+
+            @pl.when(here)
+            def _():
+                put(4 * room + k * cap + at, p)
+
+            return at + here.astype(jnp.int32)
+
+        lax.fori_loop(0, cnt[me], listed, jnp.int32(0))
+
+
+def gather_kernel(ping_dev, cap, span, local, relayed, send, echoes, halo, *refs):
+    room = 4 * cap
+    begin, n = span
+    sources = refs[: 2 * relayed]
+    outs = refs[2 * relayed : -1]
+    sems = refs[-1]
+    width = echoes.shape[2]
+    jobs = []
+    for axis in range(2):
+        for i in range(n):
+            jobs.append((axis * room + begin + i, outs[axis], i, axis))
+    if local:
+        for k in range(2):
+            for i in range(cap):
+                jobs.append((2 * room + k * cap + i, outs[2 + k], i, None))
+
+    def copies(job, number):
+        at, out, i, axis = job
+        index = send[at]
+        here = jnp.minimum(index, ping_dev - 1)
+        groups = [
+            (
+                index < ping_dev,
+                [
+                    pltpu.make_async_copy(
+                        echoes.at[here], out.at[i, :, pl.ds(0, width)], sems.at[number, 0]
+                    ),
+                    pltpu.make_async_copy(
+                        halo.at[here], out.at[i, :, pl.ds(width, LANES)], sems.at[number, 1]
+                    ),
+                ],
+            )
+        ]
+        if axis is not None:
+            for k in range(relayed):
+                low = ping_dev + k * LEAD
+                chosen = (index >= low) & (index < low + LEAD)
+                source = sources[2 * k + 1 - axis]
+                from_place = jnp.clip(index - low, 0, LEAD - 1)
+                groups.append(
+                    (chosen, [pltpu.make_async_copy(source.at[from_place], out.at[i], sems.at[number, 0])])
+                )
+        return groups
+
+    for number, job in enumerate(jobs):
+        for chosen, group in copies(job, number):
+
+            @pl.when(chosen)
+            def _(group=group):
+                for copy in group:
+                    copy.start()
+
+    for number, job in enumerate(jobs):
+        for chosen, group in copies(job, number):
+
+            @pl.when(chosen)
+            def _(group=group):
+                for copy in group:
+                    copy.wait()
+
+
+def weights_kernel(ping_dev, spacing, pixels, table, where, cnt, me_ref, out):
+    count = table.shape[0] // 3
+    me = me_ref[0]
+    step = pl.program_id(0)
+    lane = lax.broadcasted_iota(jnp.int32, (1, LANES), 1)
+    second = lane >= 2 * C
+    part = (lane // C) % 2
+    channel = lane % C
+    bases, shifts, lives = [], [], []
+    for k in range(2):
+        at = where[2 * step + k]
+        d = me * pixels - table[at] * spacing
+        bases.append(jnp.full((1, LANES), d, jnp.int32))
+        shifts.append(jnp.full((1, LANES), table[count + at], jnp.int32))
+        lives.append(jnp.full((1, LANES), table[2 * count + at], jnp.int32))
+    pick = lambda pair: jnp.where(second, pair[1], pair[0])
+    base = jnp.remainder(pick(bases) - 2 * channel, phase_modulus).astype(jnp.float32)
+    turn = pick(shifts).astype(jnp.float32) * 0.125 + part.astype(jnp.float32) * 0.25
+    amount = jnp.full((1, LANES), cnt[me], jnp.int32).astype(jnp.float32)
+    scale = pick(lives).astype(jnp.float32) / jnp.sqrt(jnp.float32(C) * amount)
+    modulus = jnp.float32(phase_modulus)
+    inverse = jnp.float32(1.0 / phase_modulus)
+    strip = 64
+    rows = lax.broadcasted_iota(jnp.int32, (strip, LANES), 0).astype(jnp.float32)
+
+    def one_strip(r, _):
+        start = pl.multiple_of(r * strip, strip)
+        m = (rows + start.astype(jnp.float32)) + base
+        m = jnp.where(m > 0.5 * phase_modulus, m - modulus, m)
+        square = m * m
+        rest = square - jnp.floor(square * inverse + 0.5) * modulus
+        g = rest * inverse + turn
+        g = g - jnp.floor(g + 0.5)
+        u = g * g
+        cosine = jnp.float32(COS_TERMS[-1])
+        for term in COS_TERMS[-2::-1]:
+            cosine = cosine * u + term
+        sine = jnp.float32(SIN_TERMS[-1])
+        for term in SIN_TERMS[-2::-1]:
+            sine = sine * u + term
+        out[pl.ds(start, strip), :] = (cosine * scale).astype(out.dtype)
+        out[pl.ds(pl.multiple_of(pixels + start, strip), strip), :] = (sine * g * scale).astype(out.dtype)
+        return 0
+
+    lax.fori_loop(0, pixels // strip, one_strip, 0)
+
+
+def focus_kernel(slots, sizes, table, where, turn, weights, *refs):
+    arrays = refs[: len(sizes)]
+    total, out, window = refs[len(sizes) :]
+    count = table.shape[0] // 3
+    width = window.shape[1]
+    blocks = width // LANES
+    rows = 16
+    column = total.shape[1]
+
+    @pl.when(pl.program_id(0) == 0)
+    def _():
+        lane = lax.broadcasted_iota(jnp.int32, (rows, LANES), 1)
+        first = 0
+        for array, size in zip(arrays, sizes):
+
+            def one_slot(i, _, array=array, first=first):
+                slot = first + i
+                at = where[slot]
+                ping = table[at]
+                offset = table[count + at]
+                cosine = turn[0, ping]
+                sine = turn[1, ping]
+                roll = (LANES - offset) & (LANES - 1)
+
+                def strip(r, _, forward):
+                    top = pl.multiple_of(r * rows, rows)
+                    place = pl.multiple_of(slot * 2 * C + r * rows, rows)
+
+                    def rolled(b):
+                        cut = pl.ds((b % (blocks + 1)) * LANES, LANES)
+                        real = array[i, pl.ds(top, rows), cut].astype(jnp.float32)
+                        imag = array[i, pl.ds(pl.multiple_of(C + top, rows), rows), cut].astype(jnp.float32)
+                        return (
+                            pltpu.roll(real * cosine + imag * sine, roll, 1),
+                            pltpu.roll(imag * cosine - real * sine, roll, 1),
+                        )
+
+                    keep = lane < LANES - offset if forward else lane >= -offset
+                    before = rolled(0 if forward else -1)
+                    for b in range(blocks):
+                        after = rolled(b + 1 if forward else b)
+                        now, beside = (before, after) if forward else (after, before)
+                        cut = pl.ds(b * LANES, LANES)
+                        window[pl.ds(place, rows), cut] = jnp.where(keep, now[0], beside[0]).astype(window.dtype)
+                        window[pl.ds(pl.multiple_of(place + C, rows), rows), cut] = jnp.where(
+                            keep, now[1], beside[1]
+                        ).astype(window.dtype)
+                        before = after
+                    return 0
+
+                @pl.when(offset >= 0)
+                def _():
+                    lax.fori_loop(0, C // rows, functools.partial(strip, forward=True), 0)
+
+                @pl.when(offset < 0)
+                def _():
+                    lax.fori_loop(0, C // rows, functools.partial(strip, forward=False), 0)
+
+                return 0
+
+            lax.fori_loop(0, size, one_slot, 0)
+            first += size
+
+    tall = total.shape[0]
+    piece = min(tall, 512)
+    here = pl.ds(pl.multiple_of(pl.program_id(0) * column, column), column)
+
+    def one_piece(r, _):
+        part = pl.ds(pl.multiple_of(r * piece, piece), piece)
+        product = jnp.dot(weights[part, :], window[:, here], preferred_element_type=jnp.float32)
+        out[part, :] = (total[part, :].astype(jnp.float32) + product).astype(out.dtype)
+        return 0
+
+    lax.fori_loop(0, tall // piece, one_piece, 0)
+
+
+def params(mib):
+    return pltpu.CompilerParams(vmem_limit_bytes=mib * MIB)
+
+
+def swap(shard, by):
+    return lax.ppermute(shard, "ping", [(i, i ^ by) for i in range(lax.axis_size("ping"))])
+
+
+def turns(echoes, pairing):
+    owners, ranges = lax.axis_size("ping"), lax.axis_size("rng")
+    channel_ids = jnp.arange(C, dtype=jnp.int32)
+    front_pick = (pairing[:, 0, :, None] == channel_ids).astype(jnp.bfloat16)
+    rear_pick = (pairing[:, 1, :, None] == channel_ids).astype(jnp.bfloat16)
+    last_ping = passed_along(echoes[-1], "ping", 1)
+    rear_rows = jnp.einsum("pkc,pzcr->pzkr", rear_pick, echoes, preferred_element_type=jnp.float32)
+    inner_rows = jnp.einsum(
+        "pkc,pzcr->pzkr", front_pick[1:], echoes[:-1], preferred_element_type=jnp.float32
+    )
+    lead_rows = jnp.einsum(
+        "kc,zcr->zkr", front_pick[0], last_ping, preferred_element_type=jnp.float32
+    )
+    front_rows = jnp.concatenate([lead_rows[None], inner_rows], axis=0)
+    cross_sum = jnp.sum(
+        front_rows[:, 0] * rear_rows[:, 1] - front_rows[:, 1] * rear_rows[:, 0], axis=(1, 2)
+    )
+    front_energy = jnp.sum(front_rows * front_rows, axis=(1, 2, 3))
+    rear_energy = jnp.sum(rear_rows * rear_rows, axis=(1, 2, 3))
+    parts = jnp.stack([cross_sum, front_energy, rear_energy])
+    every = lax.all_gather(parts, ("ping", "rng"))
+    sums = jnp.sum(every.reshape(owners, ranges, 3, -1), axis=1)
+    cross_sum, front_energy, rear_energy = [sums[:, i].reshape(-1) for i in range(3)]
+    increment = cross_sum / (jnp.sqrt(front_energy * rear_energy) + small_value)
+    order = jnp.arange(increment.shape[0], dtype=jnp.int32)
+    track_turn = jnp.sum(jnp.where(order[None, :] <= order[:, None], increment[None, :], 0.0), axis=1)
+    return jnp.stack([jnp.cos(track_turn), jnp.sin(track_turn)])
+
+
+def chunked(chunks, echoes, pairing, counts, me, flat, halo, send, table, earlier):
+    owners = lax.axis_size("ping")
+    ping_dev, channels, width = flat.shape
+    cap = -(-MOST // owners)
+    room = 4 * cap
+    wide = width + LANES
+    pixels = earlier.shape[2]
+    spacing = pixels * earlier.shape[0] // ping_dev
+    slot = lambda n: jax.ShapeDtypeStruct((n, channels, wide), flat.dtype)
+    received, groups = [], []
+    begin = 0
+    local = None
+    for c, n in enumerate(chunks):
+        relayed = min(max(c - 1, 0), 2)
+        shapes = [slot(n), slot(n)] + ([slot(cap), slot(cap)] if c == 0 else [])
+        moved = pl.pallas_call(
+            functools.partial(gather_kernel, ping_dev, cap, (begin, n), c == 0, relayed),
+            out_shape=shapes,
+            in_specs=[SMEM] + [ANY] * (2 + 2 * relayed),
+            out_specs=[ANY] * len(shapes),
+            scratch_shapes=[pltpu.SemaphoreType.DMA((2 * n + (2 * cap if c == 0 else 0), 2))],
+            cost_estimate=pl.CostEstimate(flops=0, bytes_accessed=4 * n * channels * wide * 2, transcendentals=0),
+            name="gather",
+        )(send, flat, halo, *[a for pair in received[:relayed] for a in pair])
+        over_x, over_y = swap(moved[0], 2), swap(moved[1], 4)
+        received.append((over_x, over_y))
+        arrays = [over_x, over_y, swap(over_x, 1), swap(over_y, 1)]
+        places = [a * room + begin + i for a in range(4) for i in range(n)]
+        if c == 0:
+            arrays = [moved[2], swap(moved[3], 1)] + arrays
+            places = [4 * room + i for i in range(2 * cap)] + places
+        groups.append((arrays, places))
+        begin += n
+
+    weights = []
+    for arrays, places in groups:
+        slots = len(places)
+        weights.append(
+            pl.pallas_call(
+                functools.partial(weights_kernel, ping_dev, spacing, pixels),
+                grid=(slots // 2,),
+                in_specs=[SMEM] * 4,
+                out_specs=pl.BlockSpec((2 * pixels, LANES), lambda i: (0, i)),
+                out_shape=jax.ShapeDtypeStruct((2 * pixels, slots * 2 * C), jnp.bfloat16),
+                cost_estimate=pl.CostEstimate(
+                    flops=40 * pixels * slots * 2 * C, bytes_accessed=2 * pixels * slots * 4 * C, transcendentals=0
+                ),
+                name="weights",
+            )(table, np.asarray(places, np.int32), counts, me)
+        )
+
+    turn = turns(echoes, pairing)
+    total = earlier.reshape(2 * pixels, width)
+    column = 256
+    for number, ((arrays, places), weight) in enumerate(zip(groups, weights)):
+        slots = len(places)
+        deep = slots * 2 * C
+        final = number == len(groups) - 1
+        sizes = [a.shape[0] for a in arrays]
+        kind = jnp.bfloat16 if final else jnp.float32
+        total = pl.pallas_call(
+            functools.partial(focus_kernel, slots, sizes),
+            grid=(width // column,),
+            in_specs=[SMEM, SMEM, SMEM]
+            + [pl.BlockSpec(memory_space=pltpu.VMEM)] * (1 + len(arrays))
+            + [pl.BlockSpec((2 * pixels, column), lambda i: (0, i))],
+            out_specs=pl.BlockSpec((2 * pixels, column), lambda i: (0, i)),
+            out_shape=jax.ShapeDtypeStruct((2 * pixels, width), kind),
+            scratch_shapes=[pltpu.VMEM((deep, width), jnp.bfloat16)],
+            compiler_params=params(48),
+            cost_estimate=pl.CostEstimate(
+                flops=2 * 2 * pixels * deep * width,
+                bytes_accessed=2 * pixels * width * 8 + deep * (width + 2 * pixels) * 2,
+                transcendentals=0,
+            ),
+            name="focus",
+        )(table, np.asarray(places, np.int32), turn, weight, *arrays, total)
+    return total.reshape(earlier.shape)
+
+
+def paired_device(echoes, pairing, footprint, counts, offsets, earlier):
+    owners, ranges = lax.axis_size("ping"), lax.axis_size("rng")
+    tiles = footprint.shape[0]
+    ping_dev, _, _, width = echoes.shape
+    cap = -(-MOST // owners)
+    room = 4 * cap
+    base = owners * (owners // 2)
+    count = 4 * room + 2 * cap
+    flat = echoes.reshape(ping_dev, 2 * C, width)
+    head = lax.slice_in_dim(flat, 0, LANES, axis=2)
+    tail = lax.slice_in_dim(flat, width - LANES, width, axis=2)
+    after = lax.ppermute(head, "rng", [(i + 1, i) for i in range(ranges - 1)])
+    ahead = lax.ppermute(tail, "rng", [(i, i + 1) for i in range(ranges - 1)])
+    halo = jnp.where(jnp.arange(LANES) < BAND, after, ahead)
+    me = lax.axis_index("ping").astype(jnp.int32).reshape(1)
+    whole = lambda *shape: jax.ShapeDtypeStruct(shape, jnp.int32)
+    send, masks, total = pl.pallas_call(
+        functools.partial(plan_kernel, owners, ping_dev, cap, MOST, tiles),
+        out_shape=[whole(2 * room + 2 * cap), whole(base + 2 * owners), whole(1)],
+        in_specs=[SMEM] * 3,
+        out_specs=[SMEM] * 3,
+        name="plan",
+    )(footprint, counts, me)
+    table = pl.pallas_call(
+        functools.partial(places_kernel, owners, ping_dev, cap),
+        out_shape=whole(3 * count),
+        in_specs=[SMEM] * 5,
+        out_specs=SMEM,
+        scratch_shapes=[pltpu.SMEM((owners * ping_dev,), jnp.int32)],
+        name="places",
+    )(footprint, counts, offsets, masks, me)
+    lengths = np.asarray([sum(v) for v in VARIANTS[:-1]], np.int32)
+    chosen = jnp.sum((total > lengths).astype(jnp.int32))
+    return lax.switch(
+        chosen,
+        [functools.partial(chunked, v) for v in VARIANTS],
+        echoes, pairing, counts, me, flat, halo, send, table, earlier,
+    )
+
+
+def per_device(echoes, pairing, footprint, counts, offsets, earlier):
+    owners = lax.axis_size("ping")
+    ping_dev = echoes.shape[0]
+    paired = (
+        owners == 8
+        and footprint.shape[0] == owners
+        and ping_dev <= 16
+        and ping_dev & (ping_dev - 1) == 0
+        and sum(VARIANTS[-1]) >= 4 * -(-MOST // owners)
+    )
+    device = paired_device if paired else general_device
+    return device(echoes, pairing, footprint, counts, offsets, earlier)
+
+
 def solution(mesh):
     return jax.shard_map(
         per_device,

time: 450 us -> 604 us (1.34)
  Pallas kernels: 0 us -> 481 us
  local copies, waits for them, and re-layouts: 200 us -> 4.51 us
  other arithmetic: 79.1 us -> 5.92 us
  waiting for transfers between devices: 75.1 us -> 9.8 us
  blocking collectives: 24.4 us -> 66.5 us
  matrix products: 41.5 us -> 9.59 us
  starting transfers between devices: 15.5 us -> 22 us
    pallas_call x0 -> x14, Pallas kernels: none -> 481 us  [the longest x4 331 us: chunked(): pl.pallas_call(functools.partial(gather_kernel, ping_dev, cap, (begin, n)...]
    gather x144 -> x0, local copies, waits for them, and re-layouts: 180 us -> none
    all_to_all x2 -> x0, waiting for transfers between devices: 69 us -> none  [the longest x1 69 us: per_device(): lax.all_to_all(outgoing, 'ping', split_axis=0, concat_axis=0, tiled=True)]
    another operation x6 -> x1, other arithmetic: 67.6 us -> 0.01 us  [turns(): return jnp.stack([jnp.cos(track_turn), jnp.sin(track_turn)])]
    all_gather x1, blocking collectives: 12.4 us -> 66.5 us  [turns(): every = lax.all_gather(parts, ('ping', 'rng'))]
    dot_general x4 -> x3, matrix products: 41.5 us -> 9.59 us  [the longest x1 4.24 us: turns(): jnp.einsum('pkc,pzcr->pzkr', rear_pick, echoes, preferred_element_type=jn...]
    ppermute x2 -> x19, starting transfers between devices: 2.6 us -> 19.2 us  [the longest x17 12.3 us: swap(): lax.ppermute(shard, 'ping', [(i, i ^ by) for i in range(lax.axis_size('pi...]
    psum x1 -> x0, blocking collectives: 12 us -> none  [per_device(): lax.psum((cross_sum, front_energy, rear_energy), 'rng')]
  transfers between devices with their start and end apart: 5 -> 20, of which waited for: 3 -> 1; matrix products, arithmetic and copies ran while one was open for 64% -> 3% of each run, Pallas kernels for 0% -> 50%
where the time goes in v1:
time: 604 us; the launch traced here: 600 us
  Pallas kernels  481 us (80%)
  blocking collectives  66.5 us (11%)
  starting transfers between devices  22 us (4%)
  waiting for transfers between devices  9.8 us (2%)
  matrix products  9.59 us (2%)
    pallas_call x4, Pallas kernels, chunked(): pl.pallas_call(functools.partial(gather_kernel, ping_dev, cap, (begin, n)...  331 us
    pallas_call x4, Pallas kernels, chunked(): pl.pallas_call(functools.partial(focus_kernel, slots, sizes), grid=(width...  103 us
    all_gather x1, blocking collectives, turns(): every = lax.all_gather(parts, ('ping', 'rng'))  66.5 us
    pallas_call x4, Pallas kernels, chunked(): pl.pallas_call(functools.partial(weights_kernel, ping_dev, spacing, pixel...  37.4 us
    ppermute x17, starting transfers between devices, swap(): lax.ppermute(shard, 'ping', [(i, i ^ by) for i in range(lax.axis_size('pi...  12.3 us
  transfers between devices with their start and end apart: 20, of which 1 were waited for; matrix products, arithmetic and copies ran while one was open for 3% of the time, Pallas kernels for 50%

profile of v1, /device:TPU:0, one launch (start us, length us, event | category | flops | bytes accessed | tf_op | source)
XLA Modules:
  0.0 599.8 jit_solution(15305336868415700572)
XLA Ops:
  0.0 1.1 fusion.55
  1.1 1.3 collective-permute-start.58
  2.4 5.6 collective-permute-start.59
  8.0 4.3 plan.1
  12.2 5.1 places.1
  17.4 1.9 fusion.54
  20.0 579.9 %conditional.1 = (bf16[1,2,1024,2048]{3,2,1,0:T(8,128)(2,1)}) conditional(s32[]{:T(128)} %clamp.3, (s32[16,2,8]{0,2,1:T(8,128)}, bf16[16,2,32,2048]{3,2,1,0:T(8,128)(2,1)}, s32[324]{0:T(512)S(1)}, s32[16]{0:T(128)}, s32[8]{0:T(128)}, /*index=5*/s32[1]{0:T(128)}, s32[60]{0:T(128)S(1)}, bf16[16,64,2048]{2,1,0:T(8,128)(2,1)}, ...), branch_computations={%region_1.7_spmd, %region_7.13_spmd, %region_13.19_spmd} | conditional | flops 58336534528 | bytes 499439680 | solution.py:696
  20.0 160.8 %gather.16 = (bf16[4,64,2176]{2,1,0:T(8,128)(2,1)}, bf16[4,64,2176]{2,1,0:T(8,128)(2,1)}, bf16[6,64,2176]{2,1,0:T(8,128)(2,1)}, bf16[6,64,2176]{2,1,0:T(8,128)(2,1)}) custom-call(s32[60]{0:T(128)S(1)} %get-tuple-element.145.send, bf16[16,64,2048]{2,1,0:T(8,128)(2,1)} %get-tuple-element.146.echoes, bf16[16,64,128]{2,1,0:T(8,128)(2,1)S(1)} %get-tuple-element.147.halo), custom_call_target="tpu_custom_call" | custom-call | bytes 4456448 | tf_op jit(solution)/shard_map/cond/branch_1_fun/gather/pallas_call | solution.py:598
  180.9 3.7 collective-permute-start.15
  184.6 0.4 collective-permute-start.16
  185.0 0.8 collective-permute-start.29
  185.8 65.3 %gather.17 = (bf16[4,64,2176]{2,1,0:T(8,128)(2,1)}, bf16[4,64,2176]{2,1,0:T(8,128)(2,1)}) custom-call(s32[60]{0:T(128)S(1)} %get-tuple-element.145.send, bf16[16,64,2048]{2,1,0:T(8,128)(2,1)} %get-tuple-element.146.echoes, bf16[16,64,128]{2,1,0:T(8,128)(2,1)S(1)} %get-tuple-element.147.halo), custom_call_target="tpu_custom_call" | custom-call | bytes 4456448 | tf_op jit(solution)/shard_map/cond/branch_1_fun/gather/pallas_call | solution.py:598
  251.1 0.4 collective-permute-start.17
  251.6 0.5 collective-permute-start.18
  252.1 0.1 copy.56
  252.2 4.2 multiply_reduce_fusion.1
  256.5 5.2 weights.16
  261.7 8.9 %weights.18 = bf16[2048,1024]{1,0:T(8,128)(2,1)} custom-call(s32[324]{0:T(512)S(1)} %get-tuple-element.138.table, s32[16]{0:T(128)S(1)} %copy-done.37, s32[8]{0:T(128)S(1)} %copy-done.31, s32[1]{0:T(128)} %get-tuple-element.144.me_ref), custom_call_target="tpu_custom_call" | custom-call | flops 41943040 | bytes 4194304 | tf_op jit(solution)/shard_map/cond/branch_1_fun/weights/pallas_call | solution.py:621
  270.7 8.9 %weights.17 = bf16[2048,1024]{1,0:T(8,128)(2,1)} custom-call(s32[324]{0:T(512)S(1)} %get-tuple-element.138.table, s32[16]{0:T(128)S(1)} %copy-done.40, s32[8]{0:T(128)S(1)} %copy-done.31, s32[1]{0:T(128)} %get-tuple-element.144.me_ref), custom_call_target="tpu_custom_call" | custom-call | flops 41943040 | bytes 4194304 | tf_op jit(solution)/shard_map/cond/branch_1_fun/weights/pallas_call | solution.py:621
  279.6 14.4 %weights.19 = bf16[2048,1792]{1,0:T(8,128)(2,1)} custom-call(s32[324]{0:T(512)S(1)} %get-tuple-element.138.table, s32[28]{0:T(128)S(1)} %copy-done.43, s32[8]{0:T(128)S(1)} %copy-done.31, s32[1]{0:T(128)} %get-tuple-element.144.me_ref), custom_call_target="tpu_custom_call" | custom-call | flops 73400320 | bytes 7340032 | tf_op jit(solution)/shard_map/cond/branch_1_fun/weights/pallas_call | solution.py:621
  293.9 0.1 iota_compare_fusion.4
  294.0 1.7 slice_bitcast_fusion.7
  295.7 2.8 collective-permute-start.14
  298.5 4.0 fusion.20
  302.6 69.3 %gather.19 = (bf16[4,64,2176]{2,1,0:T(8,128)(2,1)}, bf16[4,64,2176]{2,1,0:T(8,128)(2,1)}) custom-call(s32[60]{0:T(128)S(1)} %get-tuple-element.145.send, bf16[16,64,2048]{2,1,0:T(8,128)(2,1)} %get-tuple-element.146.echoes, bf16[16,64,128]{2,1,0:T(8,128)(2,1)} %copy-done.24, bf16[4,64,2176]{2,1,0:T(8,128)(2,1)} %copy-done.12, ...), custom_call_target="tpu_custom_call" | custom-call | bytes 4456448 | tf_op jit(solution)/shard_map/cond/branch_1_fun/gather/pallas_call | solution.py:598
  371.9 1.3 collective-permute-start.23
  373.2 1.2 collective-permute-start.24
  374.5 0.5 collective-permute-start.31
  374.9 1.3 convolution_bitcast_fusion.3
  376.3 1.8 fusion.24
  378.1 1.9 fusion.28
  380.0 66.5 %all-gather.4 = f32[32,3,16]{2,1,0:T(4,128)S(1)} all-gather(f32[1,3,16]{2,1,0:T(4,128)S(1)} %maximum_bitcast_fusion.1), channel_id=3, replica_groups=mesh['ping'=8,'rng'=4] {'ping','rng'}, dimensions={0}, use_global_device_ids=true | all-gather | bytes 6336 | tf_op jit(solution)/shard_map/cond/branch_1_fun/all_gather | solution.py:574
  446.6 35.5 %gather.18 = (bf16[2,64,2176]{2,1,0:T(8,128)(2,1)}, bf16[2,64,2176]{2,1,0:T(8,128)(2,1)}) custom-call(s32[60]{0:T(128)S(1)} %get-tuple-element.145.send, bf16[16,64,2048]{2,1,0:T(8,128)(2,1)} %get-tuple-element.146.echoes, bf16[16,64,128]{2,1,0:T(8,128)(2,1)} %copy-done.24, bf16[4,64,2176]{2,1,0:T(8,128)(2,1)} %copy-done.12, ...), custom_call_target="tpu_custom_call" | custom-call | bytes 2228224 | tf_op jit(solution)/shard_map/cond/branch_1_fun/gather/pallas_call | solution.py:598
  482.1 0.1 collective-permute-start.19
  482.2 0.1 div.27
  482.3 0.1 select_reduce_fusion.1
  482.4 9.8 %collective-permute-done.19.refs_0_ = bf16[2,64,2176]{2,1,0:T(8,128)(2,1)} collective-permute-done((bf16[2,64,2176]{2,1,0:T(8,128)(2,1)}, bf16[2,64,2176]{2,1,0:T(8,128)(2,1)}, u32[]{:S(2)}, u32[]{:S(2)}) %collective-permute-start.19) | collective-permute-done | bytes 557088 | tf_op jit(solution)/shard_map/cond/branch_1_fun/ppermute | solution.py:551
  492.2 1.8 collective-permute-start.20
  494.0 0.5 collective-permute-start.28
  494.5 0.1 collective-permute-start.25
  494.6 0.4 collective-permute-start.26
  495.0 1.4 copy-done.21
  496.5 35.0 %focus.16.refs_4_ = f32[2048,2048]{1,0:T(8,128)} custom-call(s32[324]{0:T(512)S(1)} %get-tuple-element.138.table, s32[28]{0:T(128)S(1)} %copy-done.43, f32[2,128]{1,0:T(2,128)S(1)} %pad_maximum_fusion.3.turn, bf16[2048,1792]{1,0:T(8,128)(2,1)} %weights.19, bf16[6,64,2176]{2,1,0:T(8,128)(2,1)S(1)} %copy-done.21, ...), custom_call_target="tpu_custom_call" | custom-call | flops 15032385536 | bytes 48234496 | tf_op jit(solution)/shard_map/cond/branch_1_fun/focus/pallas_call | solution.py:643
  531.5 0.1 collective-permute-start.21
  531.6 0.4 collective-permute-start.22
  532.0 24.8 %focus.17.refs_4_ = f32[2048,2048]{1,0:T(8,128)} custom-call(s32[324]{0:T(512)S(1)} %get-tuple-element.138.table, s32[16]{0:T(128)S(1)} %copy-done.37, f32[2,128]{1,0:T(2,128)S(1)} %pad_maximum_fusion.3.turn, bf16[2048,1024]{1,0:T(8,128)(2,1)} %weights.18, bf16[4,64,2176]{2,1,0:T(8,128)(2,1)S(1)} %copy-done.9, bf16[4,64,2176]{2,1,0:T(8,128)(2,1)S(1)} %copy-done.11, ...), custom_call_target="tpu_custom_call" | custom-call | flops 8589934592 | bytes 41943040 | tf_op jit(solution)/shard_map/cond/branch_1_fun/focus/pallas_call | solution.py:643
  556.8 25.6 %focus.18.refs_4_ = f32[2048,2048]{1,0:T(8,128)} custom-call(s32[324]{0:T(512)S(1)} %get-tuple-element.138.table, s32[16]{0:T(128)S(1)} %copy-done.40, f32[2,128]{1,0:T(2,128)S(1)} %pad_maximum_fusion.3.turn, bf16[2048,1024]{1,0:T(8,128)(2,1)} %weights.17, bf16[4,64,2176]{2,1,0:T(8,128)(2,1)} %collective-permute-done.23.refs_0_, ...), custom_call_target="tpu_custom_call" | custom-call | flops 8589934592 | bytes 41943040 | tf_op jit(solution)/shard_map/cond/branch_1_fun/focus/pallas_call | solution.py:643
  582.4 17.4 %focus.19 = bf16[2048,2048]{1,0:T(8,128)(2,1)} custom-call(s32[324]{0:T(512)S(1)} %get-tuple-element.138.table, s32[8]{0:T(128)S(1)} %copy-done.18, f32[2,128]{1,0:T(2,128)S(1)} %pad_maximum_fusion.3.turn, bf16[2048,512]{1,0:T(8,128)(2,1)S(1)} %copy-done.7, bf16[2,64,2176]{2,1,0:T(8,128)(2,1)} %collective-permute-done.19.refs_0_, ...), custom_call_target="tpu_custom_call" | custom-call | flops 4294967296 | bytes 37748736 | tf_op jit(solution)/shard_map/cond/branch_1_fun/focus/pallas_call | solution.py:643
  (61 shorter events, 0.4 us)
Async XLA Ops:
  1.1 18.8 %collective-permute-start.58 = (bf16[16,64,128]{2,1,0:T(8,128)(2,1)S(1)}, bf16[16,64,128]{2,1,0:T(8,128)(2,1)S(1)}, u32[]{:S(2)}, u32[]{:S(2)}) collective-permute-start(bf16[16,64,128]{2,1,0:T(8,128)(2,1)S(1)} %get-tuple-element.234), channel_id=1, source_target_pairs={{1,0},{2,1},{3,2},{5,4},{6,5},{7,6},{9,8},{10,9},{11,10},{13,12},{... | collective-permute-start | bytes 786440 | tf_op jit(solution)/shard_map/ppermute | solution.py:674
  2.4 17.6 %collective-permute-start.59 = (bf16[16,64,128]{2,1,0:T(8,128)(2,1)S(1)}, bf16[16,64,128]{2,1,0:T(8,128)(2,1)S(1)}, u32[]{:S(2)}, u32[]{:S(2)}) collective-permute-start(bf16[16,64,128]{2,1,0:T(8,128)(2,1)S(1)} %get-tuple-element.233), channel_id=1, source_target_pairs={{0,1},{1,2},{2,3},{4,5},{5,6},{6,7},{8,9},{9,10},{10,11},{12,13},{... | collective-permute-start | bytes 786440 | tf_op jit(solution)/shard_map/ppermute | solution.py:675
  20.0 231.1 %copy-start.24 = (bf16[16,64,128]{2,1,0:T(8,128)(2,1)}, bf16[16,64,128]{2,1,0:T(8,128)(2,1)S(1)}, u32[]{:S(2)}) copy-start(bf16[16,64,128]{2,1,0:T(8,128)(2,1)S(1)} %get-tuple-element.147.halo) | copy-start | bytes 786436 | tf_op jit(solution)/shard_map/cond
  180.9 114.8 %collective-permute-start.15 = (bf16[4,64,2176]{2,1,0:T(8,128)(2,1)}, bf16[4,64,2176]{2,1,0:T(8,128)(2,1)S(1)}, u32[]{:S(2)}, u32[]{:S(2)}) collective-permute-start(bf16[4,64,2176]{2,1,0:T(8,128)(2,1)} %get-tuple-element.148), channel_id=1, source_target_pairs={{0,8},{4,12},{8,0},{12,4},{16,24},{20,28},{24,16},{28,20},{1,9},{5... | collective-permute-start | bytes 3342344 | tf_op jit(solution)/shard_map/cond/branch_1_fun/ppermute | solution.py:551
  184.6 118.0 %collective-permute-start.16 = (bf16[4,64,2176]{2,1,0:T(8,128)(2,1)}, bf16[4,64,2176]{2,1,0:T(8,128)(2,1)}, u32[]{:S(2)}, u32[]{:S(2)}) collective-permute-start(bf16[4,64,2176]{2,1,0:T(8,128)(2,1)} %get-tuple-element.149), channel_id=1, source_target_pairs={{0,16},{4,20},{8,24},{12,28},{16,0},{20,4},{24,8},{28,12},{1,17},{... | collective-permute-start | bytes 3342344 | tf_op jit(solution)/shard_map/cond/branch_1_fun/ppermute | solution.py:551
  185.0 67.1 %copy-start.34 = (s32[16,2,8]{0,2,1:T(8,128)S(1)}, s32[16,2,8]{0,2,1:T(8,128)}, u32[]{:S(2)}) copy-start(s32[16,2,8]{0,2,1:T(8,128)} %get-tuple-element.140) | copy-start | bytes 3076 | tf_op jit(solution)/shard_map/cond
  185.0 297.0 %collective-permute-start.29 = (bf16[6,64,2176]{2,1,0:T(8,128)(2,1)}, bf16[6,64,2176]{2,1,0:T(8,128)(2,1)}, u32[]{:S(2)}, u32[]{:S(2)}) collective-permute-start(bf16[6,64,2176]{2,1,0:T(8,128)(2,1)} %get-tuple-element.163), channel_id=1, source_target_pairs={{0,4},{4,0},{8,12},{12,8},{16,20},{20,16},{24,28},{28,24},{1,5},{5... | collective-permute-start | bytes 5013512 | tf_op jit(solution)/shard_map/cond/branch_1_fun/ppermute | solution.py:551
  251.1 123.3 %collective-permute-start.17 = (bf16[4,64,2176]{2,1,0:T(8,128)(2,1)}, bf16[4,64,2176]{2,1,0:T(8,128)(2,1)S(1)}, u32[]{:S(2)}, u32[]{:S(2)}) collective-permute-start(bf16[4,64,2176]{2,1,0:T(8,128)(2,1)} %get-tuple-element.150), channel_id=1, source_target_pairs={{0,8},{4,12},{8,0},{12,4},{16,24},{20,28},{24,16},{28,20},{1,9},{5... | collective-permute-start | bytes 3342344 | tf_op jit(solution)/shard_map/cond/branch_1_fun/ppermute | solution.py:551
  251.6 122.9 %collective-permute-start.18 = (bf16[4,64,2176]{2,1,0:T(8,128)(2,1)}, bf16[4,64,2176]{2,1,0:T(8,128)(2,1)S(1)}, u32[]{:S(2)}, u32[]{:S(2)}) collective-permute-start(bf16[4,64,2176]{2,1,0:T(8,128)(2,1)} %get-tuple-element.151), channel_id=1, source_target_pairs={{0,16},{4,20},{8,24},{12,28},{16,0},{20,4},{24,8},{28,12},{1,17},{... | collective-permute-start | bytes 3342344 | tf_op jit(solution)/shard_map/cond/branch_1_fun/ppermute | solution.py:551
  252.2 4.3 copy-start.31
  256.4 5.3 copy-start.37
  261.7 8.9 %copy-start.40 = (s32[16]{0:T(128)S(1)}, s32[16]{0:T(128)}, u32[]{:S(2)}) copy-start(s32[16]{0:T(128)} %get-tuple-element.154.where) | copy-start | bytes 196 | tf_op jit(solution)/shard_map/cond
  270.7 8.9 %copy-start.43 = (s32[28]{0:T(128)S(1)}, s32[28]{0:T(128)}, u32[]{:S(2)}) copy-start(s32[28]{0:T(128)} %get-tuple-element.160.where) | copy-start | bytes 340 | tf_op jit(solution)/shard_map/cond
  295.7 6.9 %copy-start.12 = (bf16[4,64,2176]{2,1,0:T(8,128)(2,1)}, bf16[4,64,2176]{2,1,0:T(8,128)(2,1)S(1)}, u32[]{:S(2)}) copy-start(bf16[4,64,2176]{2,1,0:T(8,128)(2,1)S(1)} %collective-permute-done.15.refs_0_.refs_2_) | copy-start | bytes 3342340 | tf_op jit(solution)/shard_map/cond
  295.7 77.5 %collective-permute-start.14 = (bf16[2,32,2048]{2,1,0:T(8,128)(2,1)}, bf16[2,32,2048]{2,1,0:T(8,128)(2,1)}, u32[]{:S(2)}, u32[]{:S(2)}) collective-permute-start(bf16[2,32,2048]{2,1,0:T(8,128)(2,1)} %slice_bitcast_fusion.7), channel_id=1, source_target_pairs={{0,4},{4,8},{8,12},{12,16},{16,20},{20,24},{24,28},{1,5},{5,9},{9,... | collective-permute-start | bytes 786440 | tf_op jit(solution)/shard_map/cond/branch_1_fun/ppermute | solution.py:27
  371.9 6.2 %copy-start.29 = (f32[15,2,8,2048]{3,2,1,0:T(8,128)S(1)}, f32[15,2,8,2048]{3,2,1,0:T(8,128)}, u32[]{:S(2)}) copy-start(f32[15,2,8,2048]{3,2,1,0:T(8,128)} %fusion.20) | copy-start | bytes 5898244 | tf_op jit(solution)/shard_map/cond
  371.9 122.6 %collective-permute-start.23 = (bf16[4,64,2176]{2,1,0:T(8,128)(2,1)}, bf16[4,64,2176]{2,1,0:T(8,128)(2,1)}, u32[]{:S(2)}, u32[]{:S(2)}) collective-permute-start(bf16[4,64,2176]{2,1,0:T(8,128)(2,1)} %get-tuple-element.156), channel_id=1, source_target_pairs={{0,8},{4,12},{8,0},{12,4},{16,24},{20,28},{24,16},{28,20},{1,9},{5... | collective-permute-start | bytes 3342344 | tf_op jit(solution)/shard_map/cond/branch_1_fun/ppermute | solution.py:551
  373.2 121.4 %collective-permute-start.24 = (bf16[4,64,2176]{2,1,0:T(8,128)(2,1)}, bf16[4,64,2176]{2,1,0:T(8,128)(2,1)}, u32[]{:S(2)}, u32[]{:S(2)}) collective-permute-start(bf16[4,64,2176]{2,1,0:T(8,128)(2,1)} %get-tuple-element.157), channel_id=1, source_target_pairs={{0,16},{4,20},{8,24},{12,28},{16,0},{20,4},{24,8},{28,12},{1,17},{... | collective-permute-start | bytes 3342344 | tf_op jit(solution)/shard_map/cond/branch_1_fun/ppermute | solution.py:551
  374.4 5.6 copy-start.8
  374.4 119.6 %collective-permute-start.30 = (bf16[4,64,2176]{2,1,0:T(8,128)(2,1)}, bf16[4,64,2176]{2,1,0:T(8,128)(2,1)}, u32[]{:S(2)}, u32[]{:S(2)}) collective-permute-start(bf16[4,64,2176]{2,1,0:T(8,128)(2,1)} %copy-done.12), channel_id=1, source_target_pairs={{0,4},{4,0},{8,12},{12,8},{16,20},{20,16},{24,28},{28,24},{1,5},{5... | collective-permute-start | bytes 3342344 | tf_op jit(solution)/shard_map/cond/branch_1_fun/ppermute | solution.py:551
  374.4 5.6 copy-start.10
  374.5 119.5 %collective-permute-start.31 = (bf16[4,64,2176]{2,1,0:T(8,128)(2,1)}, bf16[4,64,2176]{2,1,0:T(8,128)(2,1)}, u32[]{:S(2)}, u32[]{:S(2)}) collective-permute-start(bf16[4,64,2176]{2,1,0:T(8,128)(2,1)} %collective-permute-done.16.refs_1_.refs_3_), channel_id=1, source_target_pairs={{0,4},{4,0},{8,12},{12,8},{16,20},{20,16},{24,28},{28,24},{1,5},{5... | collective-permute-start | bytes 3342344 | tf_op jit(solution)/shard_map/cond/branch_1_fun/ppermute | solution.py:551
  446.5 47.5 %copy-start.9 = (bf16[4,64,2176]{2,1,0:T(8,128)(2,1)S(1)}, bf16[4,64,2176]{2,1,0:T(8,128)(2,1)}, u32[]{:S(2)}) copy-start(bf16[4,64,2176]{2,1,0:T(8,128)(2,1)} %copy-done.8) | copy-start | bytes 3342340 | tf_op jit(solution)/shard_map/cond
  446.5 47.5 %copy-start.11 = (bf16[4,64,2176]{2,1,0:T(8,128)(2,1)S(1)}, bf16[4,64,2176]{2,1,0:T(8,128)(2,1)}, u32[]{:S(2)}) copy-start(bf16[4,64,2176]{2,1,0:T(8,128)(2,1)} %copy-done.10) | copy-start | bytes 3342340 | tf_op jit(solution)/shard_map/cond
  446.6 48.5 %copy-start.13 = (bf16[4,64,2176]{2,1,0:T(8,128)(2,1)S(1)}, bf16[4,64,2176]{2,1,0:T(8,128)(2,1)}, u32[]{:S(2)}) copy-start(bf16[4,64,2176]{2,1,0:T(8,128)(2,1)} %copy-done.12) | copy-start | bytes 3342340 | tf_op jit(solution)/shard_map/cond
  482.1 10.1 %collective-permute-start.19 = (bf16[2,64,2176]{2,1,0:T(8,128)(2,1)}, bf16[2,64,2176]{2,1,0:T(8,128)(2,1)}, u32[]{:S(2)}, u32[]{:S(2)}) collective-permute-start(bf16[2,64,2176]{2,1,0:T(8,128)(2,1)} %get-tuple-element.152), channel_id=1, source_target_pairs={{0,8},{4,12},{8,0},{12,4},{16,24},{20,28},{24,16},{28,20},{1,9},{5... | collective-permute-start | bytes 1671176 | tf_op jit(solution)/shard_map/cond/branch_1_fun/ppermute | solution.py:551
  492.2 39.3 %collective-permute-start.20 = (bf16[2,64,2176]{2,1,0:T(8,128)(2,1)}, bf16[2,64,2176]{2,1,0:T(8,128)(2,1)S(1)}, u32[]{:S(2)}, u32[]{:S(2)}) collective-permute-start(bf16[2,64,2176]{2,1,0:T(8,128)(2,1)} %get-tuple-element.153), channel_id=1, source_target_pairs={{0,16},{4,20},{8,24},{12,28},{16,0},{20,4},{24,8},{28,12},{1,17},{... | collective-permute-start | bytes 1671176 | tf_op jit(solution)/shard_map/cond/branch_1_fun/ppermute | solution.py:551
  494.0 37.6 %collective-permute-start.27 = (bf16[4,64,2176]{2,1,0:T(8,128)(2,1)S(1)}, bf16[4,64,2176]{2,1,0:T(8,128)(2,1)S(1)}, u32[]{:S(2)}, u32[]{:S(2)}) collective-permute-start(bf16[4,64,2176]{2,1,0:T(8,128)(2,1)S(1)} %copy-done.9), channel_id=1, source_target_pairs={{0,4},{4,0},{8,12},{12,8},{16,20},{20,16},{24,28},{28,24},{1,5},{5... | collective-permute-start | bytes 3342344 | tf_op jit(solution)/shard_map/cond/branch_1_fun/ppermute | solution.py:551
  494.0 38.0 %collective-permute-start.28 = (bf16[4,64,2176]{2,1,0:T(8,128)(2,1)S(1)}, bf16[4,64,2176]{2,1,0:T(8,128)(2,1)S(1)}, u32[]{:S(2)}, u32[]{:S(2)}) collective-permute-start(bf16[4,64,2176]{2,1,0:T(8,128)(2,1)S(1)} %copy-done.11), channel_id=1, source_target_pairs={{0,4},{4,0},{8,12},{12,8},{16,20},{20,16},{24,28},{28,24},{1,5},{5... | collective-permute-start | bytes 3342344 | tf_op jit(solution)/shard_map/cond/branch_1_fun/ppermute | solution.py:551
  494.5 62.3 %collective-permute-start.25 = (bf16[4,64,2176]{2,1,0:T(8,128)(2,1)}, bf16[4,64,2176]{2,1,0:T(8,128)(2,1)S(1)}, u32[]{:S(2)}, u32[]{:S(2)}) collective-permute-start(bf16[4,64,2176]{2,1,0:T(8,128)(2,1)} %collective-permute-done.23.refs_0_), channel_id=1, source_target_pairs={{0,4},{4,0},{8,12},{12,8},{16,20},{20,16},{24,28},{28,24},{1,5},{5... | collective-permute-start | bytes 3342344 | tf_op jit(solution)/shard_map/cond/branch_1_fun/ppermute | solution.py:551
  494.6 62.2 %collective-permute-start.26 = (bf16[4,64,2176]{2,1,0:T(8,128)(2,1)}, bf16[4,64,2176]{2,1,0:T(8,128)(2,1)S(1)}, u32[]{:S(2)}, u32[]{:S(2)}) collective-permute-start(bf16[4,64,2176]{2,1,0:T(8,128)(2,1)} %collective-permute-done.24.refs_1_), channel_id=1, source_target_pairs={{0,4},{4,0},{8,12},{12,8},{16,20},{20,16},{24,28},{28,24},{1,5},{5... | collective-permute-start | bytes 3342344 | tf_op jit(solution)/shard_map/cond/branch_1_fun/ppermute | solution.py:551
  495.0 1.4 copy-start.21
  531.5 50.9 %collective-permute-start.21 = (bf16[2,64,2176]{2,1,0:T(8,128)(2,1)}, bf16[2,64,2176]{2,1,0:T(8,128)(2,1)S(1)}, u32[]{:S(2)}, u32[]{:S(2)}) collective-permute-start(bf16[2,64,2176]{2,1,0:T(8,128)(2,1)} %collective-permute-done.19.refs_0_), channel_id=1, source_target_pairs={{0,4},{4,0},{8,12},{12,8},{16,20},{20,16},{24,28},{28,24},{1,5},{5... | collective-permute-start | bytes 1671176 | tf_op jit(solution)/shard_map/cond/branch_1_fun/ppermute | solution.py:551
  531.6 50.8 %collective-permute-start.22 = (bf16[2,64,2176]{2,1,0:T(8,128)(2,1)S(1)}, bf16[2,64,2176]{2,1,0:T(8,128)(2,1)S(1)}, u32[]{:S(2)}, u32[]{:S(2)}) collective-permute-start(bf16[2,64,2176]{2,1,0:T(8,128)(2,1)S(1)} %collective-permute-done.20.refs_1_), channel_id=1, source_target_pairs={{0,4},{4,0},{8,12},{12,8},{16,20},{20,16},{24,28},{28,24},{1,5},{5... | collective-permute-start | bytes 1671176 | tf_op jit(solution)/shard_map/cond/branch_1_fun/ppermute | solution.py:551
  556.8 25.6 %copy-start.7 = (bf16[2048,512]{1,0:T(8,128)(2,1)S(1)}, bf16[2048,512]{1,0:T(8,128)(2,1)}, u32[]{:S(2)}) copy-start(bf16[2048,512]{1,0:T(8,128)(2,1)} %weights.16) | copy-start | bytes 6291460 | tf_op jit(solution)/shard_map/cond
  556.8 25.6 %copy-start.18 = (s32[8]{0:T(128)S(1)}, s32[8]{0:T(128)}, u32[]{:S(2)}) copy-start(s32[8]{0:T(128)} %constant.44.clone.1.where) | copy-start | bytes 100 | tf_op jit(solution)/shard_map/cond

commit v2 on v0

--- a/solution.py
+++ b/solution.py
@@ -1,8 +1,12 @@
+import functools
 import math
 
 import jax
 import jax.numpy as jnp
+import numpy as np
 from jax import lax
+from jax.experimental import pallas as pl
+from jax.experimental.pallas import tpu as pltpu
 from jax.sharding import PartitionSpec as P
 
 C = 32
@@ -96,7 +100,7 @@
     return jnp.stack(results, axis=0)
 
 
-def per_device(echoes, pairing, footprint, counts, offsets, earlier):
+def general_device(echoes, pairing, footprint, counts, offsets, earlier):
     ping_dev = echoes.shape[0]
     owners = lax.axis_size("ping")
     own_index = lax.axis_index("ping")
@@ -166,6 +170,572 @@
     return (earlier.astype(jnp.float32) + contribution).astype(jnp.bfloat16)
 
 
+LEAD = 4
+VARIANTS = ((4, 4, 4), (4, 4, 4, 2), (4, 4, 4, 4, 4, 4))
+LANES = 128
+SMALL = pl.CostEstimate(flops=1024, bytes_accessed=1024, transcendentals=0)
+MIB = 1 << 20
+COLUMN = 512
+PIECE = 1024
+FOCUS_MIB = 40
+SMEM = pl.BlockSpec(memory_space=pltpu.SMEM)
+ANY = pl.BlockSpec(memory_space=pl.ANY)
+VMEM = pl.BlockSpec(memory_space=pltpu.VMEM)
+COS_TERMS = (
+    1.0, -19.73920440673828, 64.93911743164062, -85.45014190673828, 60.16762924194336,
+    -25.967599868774414, 6.528658390045166,
+)
+SIN_TERMS = (
+    6.2831854820251465, -41.34170150756836, 81.60513305664062, -76.70301818847656, 42.02592849731445,
+    -14.899847030639648, 3.2381374835968018,
+)
+
+
+def bit_count(mask):
+    down = lax.shift_right_logical
+    mask = mask - (down(mask, 1) & 0x55555555)
+    mask = (mask & 0x33333333) + (down(mask, 2) & 0x33333333)
+    mask = (mask + down(mask, 4)) & 0x0F0F0F0F
+    mask = mask + down(mask, 8)
+    return (mask + down(mask, 16)) & 0x3F
+
+
+def each_bit(mask, place, visit):
+    def body(_, carry):
+        left, at = carry
+        low = left & -left
+        visit(at, bit_count(low - 1))
+        return left ^ low, at + 1
+
+    return lax.fori_loop(0, bit_count(mask), body, (mask, place))[1]
+
+
+def link_list(masks, owners, s, axis, own, relay):
+    chips = owners // 2
+    near, other = (1, 4) if axis == 0 else (2, 2)
+    base = owners * chips
+    chip = s >> 1
+    behind = s ^ other
+    place = each_bit(masks[base + axis * owners + s], jnp.int32(0), lambda at, bit: own(at, chip ^ 3, bit))
+    place = each_bit(masks[s * chips + (chip ^ near)], place, lambda at, bit: own(at, chip ^ near, bit))
+    begin = jnp.maximum(place, 2 * LEAD)
+    passed = masks[base + (1 - axis) * owners + behind]
+    each_bit(passed, begin, lambda at, bit: relay(at, behind, chip ^ near, bit, at - begin))
+
+
+def plan_kernel(owners, ping_dev, cap, tiles, fp, cnt, off, me_ref, send, masks, shifts, total):
+    chips = owners // 2
+    bits = ping_dev.bit_length() - 1
+    room = 4 * cap
+    base = owners * chips
+    pings = owners * ping_dev
+    places = 2 * room + 2 * cap
+    me = me_ref[0]
+
+    def clear(i, _):
+        masks[i] = 0
+        return 0
+
+    lax.fori_loop(0, base, clear, 0, unroll=8)
+
+    def clear_send(i, _):
+        send[i] = 0
+        return 0
+
+    lax.fori_loop(0, 2 * places, clear_send, 0, unroll=12)
+
+    def one_tile(t, _):
+        def entry(j, _):
+            p = fp[t, j]
+            at = (p >> bits) * chips + (t >> 1)
+            masks[at] = masks[at] | lax.shift_left(jnp.int32(1), (p & (ping_dev - 1)) + (t & 1) * ping_dev)
+            shifts[t * pings + p] = off[t, j]
+            return 0
+
+        return lax.fori_loop(0, cnt[t], entry, 0)
+
+    lax.fori_loop(0, tiles, one_tile, 0)
+
+    def split(s, _):
+        chip = s >> 1
+        far = masks[s * chips + (chip ^ 3)]
+        n = bit_count(far)
+        over_y = bit_count(masks[(s ^ 2) * chips + (chip ^ 3)])
+        over_x = bit_count(masks[(s ^ 4) * chips + (chip ^ 3)])
+        want = (n + over_x - over_y + 1) >> 1
+        want = jnp.minimum(jnp.maximum(want, jnp.maximum(n - cap, 0)), jnp.minimum(n, cap))
+
+        def take(_, carry):
+            left, taken = carry
+            low = left & -left
+            return left ^ low, taken | low
+
+        left, taken = lax.fori_loop(0, want, take, (far, jnp.int32(0)))
+        masks[base + s] = taken
+        masks[base + owners + s] = left
+        return 0
+
+    lax.fori_loop(0, owners, split, 0)
+
+    def longest(s, most_yet):
+        for axis, near, other in ((0, 1, 4), (1, 2, 2)):
+            own = bit_count(masks[base + axis * owners + s]) + bit_count(masks[s * chips + ((s >> 1) ^ near)])
+            passed = bit_count(masks[base + (1 - axis) * owners + (s ^ other)])
+            length = jnp.where(passed > 0, jnp.maximum(own, 2 * LEAD) + passed, own)
+            most_yet = jnp.maximum(most_yet, length)
+        return most_yet
+
+    length = lax.fori_loop(0, owners, longest, jnp.int32(0))
+    chosen = jnp.int32(0)
+    for variant in VARIANTS[:-1]:
+        chosen = chosen + (length > sum(variant)).astype(jnp.int32)
+    total[0] = chosen
+
+    for axis in range(2):
+
+        def own(at, chip, bit, axis=axis):
+            ping = bit & (ping_dev - 1)
+            tile = 2 * chip + (bit >> bits)
+            send[axis * room + at] = ping
+            send[places + axis * room + at] = shifts[tile * pings + me * ping_dev + ping]
+
+        def relay(at, behind, chip, bit, i, axis=axis):
+            send[axis * room + at] = ping_dev + i
+
+        link_list(masks, owners, me, axis, own, relay)
+
+    for k, tile in ((0, me), (1, me ^ 1)):
+
+        def mine(j, at, k=k, tile=tile):
+            p = fp[tile, j]
+            here = (p >> bits) == me
+
+            @pl.when(here)
+            def _():
+                send[2 * room + k * cap + at] = p & (ping_dev - 1)
+                send[places + 2 * room + k * cap + at] = off[tile, j]
+
+            return at + here.astype(jnp.int32)
+
+        lax.fori_loop(0, cnt[tile], mine, jnp.int32(0))
+
+
+def places_kernel(owners, ping_dev, cap, fp, cnt, off, masks, shifts, me_ref, table):
+    bits = ping_dev.bit_length() - 1
+    room = 4 * cap
+    count = 4 * room + 2 * cap
+    pings = owners * ping_dev
+    me = me_ref[0]
+
+    def clear(i, _):
+        table[i] = 0
+        return 0
+
+    lax.fori_loop(0, 3 * count, clear, 0, unroll=12)
+
+    def put(at, tile, ping):
+        @pl.when(tile == me)
+        def _():
+            table[at] = ping
+            table[count + at] = shifts[tile * pings + ping]
+            table[2 * count + at] = 1
+
+    for a, (axis, flip) in enumerate(((0, 2), (1, 4), (0, 3), (1, 5))):
+        s = me ^ flip
+
+        def own(at, chip, bit, a=a, s=s):
+            put(a * room + at, 2 * chip + (bit >> bits), s * ping_dev + (bit & (ping_dev - 1)))
+
+        def relay(at, behind, chip, bit, i, a=a):
+            put(a * room + at, 2 * chip + (bit >> bits), behind * ping_dev + (bit & (ping_dev - 1)))
+
+        link_list(masks, owners, s, axis, own, relay)
+
+    for k, s in ((0, me), (1, me ^ 1)):
+
+        def listed(j, at, k=k, s=s):
+            p = fp[me, j]
+            here = (p >> bits) == s
+
+            @pl.when(here)
+            def _():
+                put(4 * room + k * cap + at, me, p)
+
+            return at + here.astype(jnp.int32)
+
+        lax.fori_loop(0, cnt[me], listed, jnp.int32(0))
+
+
+def gather_kernel(ping_dev, places, spans, send, echoes, halo, *refs):
+    outs, stage, sems = refs[-len(spans) - 2 : -2], refs[-2], refs[-1]
+    sources = refs[: -len(spans) - 2]
+    width = echoes.shape[2]
+    blocks = width // LANES
+    lane = lax.broadcasted_iota(jnp.int32, (2 * C, LANES), 1)
+    jobs = [(begin + i, out, i, axis) for (begin, n, axis), out in zip(spans, outs) for i in range(n)]
+
+    def copies(number):
+        at, out, i, axis = jobs[number]
+        index = send[at]
+        here = jnp.minimum(index, ping_dev - 1)
+        plain = [
+            pltpu.make_async_copy(echoes.at[here], stage.at[number, :, pl.ds(0, width)], sems.at[number, 0]),
+            pltpu.make_async_copy(halo.at[here], stage.at[number, :, pl.ds(width, LANES)], sems.at[number, 1]),
+        ]
+        if not sources:
+            return [(None, plain)]
+        groups = [(index < ping_dev, plain)]
+        for k in range(len(sources) // 2):
+            low = ping_dev + k * LEAD
+            chosen = (index >= low) & (index < low + LEAD)
+            source = sources[2 * k + 1 - axis].at[jnp.clip(index - low, 0, LEAD - 1)]
+            groups.append((chosen, [pltpu.make_async_copy(source, out.at[i], sems.at[number, 0])]))
+        return groups
+
+    def act_on(number, act):
+        for chosen, group in copies(number):
+            if chosen is None:
+                for copy in group:
+                    act(copy)
+            else:
+
+                @pl.when(chosen)
+                def _(group=group):
+                    for copy in group:
+                        act(copy)
+
+    for number in range(len(jobs)):
+        act_on(number, lambda copy: copy.start())
+    for number in range(len(jobs)):
+        act_on(number, lambda copy: copy.wait())
+
+    number = 0
+    for (begin, n, _), out in zip(spans, outs):
+
+        def cut(i, _, begin=begin, out=out, number=number):
+            offset = send[places + begin + i]
+            within = offset & (LANES - 1)
+            roll = (LANES - within) & (LANES - 1)
+            keep = lane < LANES - within
+            low = jnp.where(offset < 0, -LANES, 0)
+
+            def rolled(b):
+                start = low + b * LANES
+                if b == 0:
+                    start = jnp.where(start < 0, width, start)
+                span = pl.ds(pl.multiple_of(start, LANES), LANES)
+                return pltpu.roll(stage[number + i, :, span].astype(jnp.float32), roll, 1)
+
+            @pl.when(send[begin + i] < ping_dev)
+            def _():
+                before = rolled(0)
+                for b in range(blocks):
+                    following = rolled(b + 1)
+                    out[i, :, pl.ds(b * LANES, LANES)] = jnp.where(keep, before, following).astype(out.dtype)
+                    before = following
+
+            return 0
+
+        lax.fori_loop(0, n, cut, 0)
+        number += n
+
+
+def turned(turn):
+    g = turn - jnp.floor(turn + 0.5)
+    u = g * g
+    cosine = jnp.full_like(u, COS_TERMS[-1])
+    for term in COS_TERMS[-2::-1]:
+        cosine = cosine * u + term
+    sine = jnp.full_like(u, SIN_TERMS[-1])
+    for term in SIN_TERMS[-2::-1]:
+        sine = sine * u + term
+    return cosine, sine * g
+
+
+def residue(number):
+    modulus = jnp.float32(phase_modulus)
+    return number - jnp.floor(number * jnp.float32(1.0 / phase_modulus) + 0.5) * modulus
+
+
+def weights_kernel(spacing, pixels, table, where, cnt, me_ref, turn_ref, out, chirp):
+    count = table.shape[0] // 3
+    me = me_ref[0]
+    step = pl.program_id(0)
+    strip = 64
+    strips = pixels // strip
+    pairs = out.shape[1] // LANES
+    inverse = jnp.float32(1.0 / phase_modulus)
+
+    def rows_of(height):
+        return lax.broadcasted_iota(jnp.int32, (height, LANES), 0).astype(jnp.float32)
+
+    @pl.when(step == 0)
+    def _():
+        def one_strip(r, _):
+            start = pl.multiple_of(r * strip, strip)
+            x = residue(rows_of(strip) + start.astype(jnp.float32))
+            cosine, sine = turned(residue(x * x) * inverse)
+            chirp[0, pl.ds(start, strip), :] = cosine
+            chirp[1, pl.ds(start, strip), :] = sine
+            return 0
+
+        lax.fori_loop(0, strips, one_strip, 0)
+
+    lane = lax.broadcasted_iota(jnp.int32, (1, LANES), 1)
+    second = lane >= 2 * C
+    part = (lane // C) % 2
+    channel = lane % C
+    amount = jnp.full((1, LANES), cnt[me], jnp.int32).astype(jnp.float32)
+    root = jnp.sqrt(jnp.float32(C) * amount)
+    far = residue(rows_of(strips) * (2.0 * strip))
+    for pair in range(pairs):
+        bases, shifts, lives, backs = [], [], [], []
+        for k in range(2):
+            at = where[2 * (pairs * step + pair) + k]
+            ping = table[at]
+            bases.append(jnp.full((1, LANES), me * pixels - ping * spacing, jnp.int32))
+            shifts.append(jnp.full((1, LANES), table[count + at], jnp.int32))
+            lives.append(jnp.full((1, LANES), table[2 * count + at], jnp.int32))
+            backs.append(jnp.full((1, LANES), turn_ref[ping], jnp.float32))
+        pick = lambda both: jnp.where(second, both[1], both[0])
+        base = residue(jnp.remainder(pick(bases) - 2 * channel, phase_modulus).astype(jnp.float32))
+        turn = pick(shifts).astype(jnp.float32) * 0.125 + part.astype(jnp.float32) * 0.25
+        scale = pick(lives).astype(jnp.float32) / root
+        inner_real, inner_imag = turned(residue(2.0 * rows_of(strip) * base) * inverse)
+        outer = residue(residue(far * base) + residue(base * base))
+        outer_real, outer_imag = turned((outer * inverse + turn) - pick(backs))
+        outer_real, outer_imag = outer_real * scale, outer_imag * scale
+        column = pl.ds(pair * LANES, LANES)
+        for s in range(strips):
+            real, imag = outer_real[s : s + 1], outer_imag[s : s + 1]
+            mid_real = inner_real * real - inner_imag * imag
+            mid_imag = inner_real * imag + inner_imag * real
+            here = pl.ds(s * strip, strip)
+            chirp_real, chirp_imag = chirp[0, here, :], chirp[1, here, :]
+            low = pl.ds(pixels + s * strip, strip)
+            out[here, column] = (mid_real * chirp_real - mid_imag * chirp_imag).astype(out.dtype)
+            out[low, column] = (mid_real * chirp_imag + mid_imag * chirp_real).astype(out.dtype)
+
+
+def focus_kernel(sizes, weights, *refs):
+    arrays = refs[: len(sizes)]
+    total, out, window = refs[len(sizes) :]
+    column = window.shape[1]
+    here = pl.ds(pl.multiple_of(pl.program_id(0) * column, column), column)
+    first = 0
+    for array, size in zip(arrays, sizes):
+        for i in range(size):
+            window[pl.ds((first + i) * 2 * C, 2 * C), :] = array[i, :, here]
+        first += size
+
+    tall = weights.shape[0]
+    piece = min(tall, PIECE)
+
+    def one_piece(r, _):
+        part = pl.ds(pl.multiple_of(r * piece, piece), piece)
+        product = jnp.dot(weights[part, :], window[...], preferred_element_type=jnp.float32)
+        out[part, :] = (total[part, :].astype(jnp.float32) + product).astype(out.dtype)
+        return 0
+
+    lax.fori_loop(0, tall // piece, one_piece, 0)
+
+
+def params(mib):
+    return pltpu.CompilerParams(vmem_limit_bytes=mib * MIB)
+
+
+def swap(shard, by):
+    return lax.ppermute(shard, "ping", [(i, i ^ by) for i in range(lax.axis_size("ping"))])
+
+
+def after(value, *others):
+    return lax.optimization_barrier((value, others))[0]
+
+
+def exchanged(echoes, pairing, last_ping):
+    owners, ranges = lax.axis_size("ping"), lax.axis_size("rng")
+    channel_ids = jnp.arange(C, dtype=jnp.int32)
+    front_pick = (pairing[:, 0, :, None] == channel_ids).astype(jnp.bfloat16)
+    rear_pick = (pairing[:, 1, :, None] == channel_ids).astype(jnp.bfloat16)
+    rear_rows = jnp.einsum("pkc,pzcr->pzkr", rear_pick, echoes, preferred_element_type=jnp.float32)
+    inner_rows = jnp.einsum(
+        "pkc,pzcr->pzkr", front_pick[1:], echoes[:-1], preferred_element_type=jnp.float32
+    )
+    lead_rows = jnp.einsum(
+        "kc,zcr->zkr", front_pick[0], last_ping, preferred_element_type=jnp.float32
+    )
+    front_rows = jnp.concatenate([lead_rows[None], inner_rows], axis=0)
+    cross_sum = jnp.sum(
+        front_rows[:, 0] * rear_rows[:, 1] - front_rows[:, 1] * rear_rows[:, 0], axis=(1, 2)
+    )
+    front_energy = jnp.sum(front_rows * front_rows, axis=(1, 2, 3))
+    rear_energy = jnp.sum(rear_rows * rear_rows, axis=(1, 2, 3))
+    parts = jnp.stack([cross_sum, front_energy, rear_energy])
+    if ranges & (ranges - 1):
+        parts = lax.psum(parts, "rng")
+    else:
+        by = 1
+        while by < ranges:
+            parts = parts + lax.ppermute(parts, "rng", [(i, i ^ by) for i in range(ranges)])
+            by *= 2
+    mine = jnp.arange(owners, dtype=jnp.int32)[:, None] == lax.axis_index("ping")
+    every = jnp.where(mine, parts[:, None, :], 0.0)
+    return every + swap(every, 1)
+
+
+def turns(every):
+    every = every + (swap(every, 2) + (swap(every, 4) + swap(every, 6)))
+    cross_sum, front_energy, rear_energy = every.reshape(3, -1)
+    increment = cross_sum / (jnp.sqrt(front_energy * rear_energy) + small_value)
+    order = jnp.arange(increment.shape[0], dtype=jnp.int32)
+    track_turn = jnp.sum(jnp.where(order[None, :] <= order[:, None], increment[None, :], 0.0), axis=1)
+    turn = track_turn * (1.0 / (2.0 * math.pi))
+    return turn - jnp.floor(turn + 0.5)
+
+
+def gather(send, flat, halo, spans, relayed=()):
+    ping_dev, channels, width = flat.shape
+    total = sum(n for _, n, _ in spans)
+    return pl.pallas_call(
+        functools.partial(gather_kernel, ping_dev, send.shape[0] // 2, spans),
+        out_shape=[jax.ShapeDtypeStruct((n, channels, width), flat.dtype) for _, n, _ in spans],
+        in_specs=[SMEM] + [ANY] * (2 + 2 * len(relayed)),
+        out_specs=[VMEM] * len(spans),
+        scratch_shapes=[
+            pltpu.VMEM((total, channels, width + LANES), flat.dtype),
+            pltpu.SemaphoreType.DMA((total, 2)),
+        ],
+        compiler_params=params(16),
+        cost_estimate=SMALL,
+        name="gather",
+    )(send, flat, halo, *[a for pair in relayed for a in pair])
+
+
+def chunked(chunks, counts, me, flat, halo, send, table, turn, moved, received, own, sibling, earlier):
+    owners = lax.axis_size("ping")
+    ping_dev, channels, width = flat.shape
+    cap = -(-MOST // owners)
+    room = 4 * cap
+    pixels = earlier.shape[2]
+    spacing = pixels * earlier.shape[0] // ping_dev
+
+    def weights_of(places):
+        slots = len(places)
+        lanes = 2 * LANES if slots % 4 == 0 else LANES
+        return pl.pallas_call(
+            functools.partial(weights_kernel, spacing, pixels),
+            grid=(slots * 2 * C // lanes,),
+            in_specs=[SMEM] * 5,
+            out_specs=pl.BlockSpec((2 * pixels, lanes), lambda i: (0, i)),
+            out_shape=jax.ShapeDtypeStruct((2 * pixels, slots * 2 * C), jnp.bfloat16),
+            scratch_shapes=[pltpu.VMEM((2, pixels, LANES), jnp.float32)],
+            cost_estimate=SMALL,
+            name="weights",
+        )(table, np.asarray(places, np.int32), counts, me, turn)
+
+    tile = pl.BlockSpec((2 * pixels, COLUMN), lambda i: (0, i))
+    tiles = width // COLUMN
+    inner = pl.BlockSpec((None, 2 * pixels, COLUMN), lambda i: (i, 0, 0))
+
+    def focus(total, arrays, weight, final):
+        sizes = [a.shape[0] for a in arrays]
+        return pl.pallas_call(
+            functools.partial(focus_kernel, sizes),
+            grid=(tiles,),
+            in_specs=[VMEM] * (1 + len(arrays)) + [tile if total.ndim == 2 else inner],
+            out_specs=tile if final else inner,
+            out_shape=jax.ShapeDtypeStruct((2 * pixels, width), earlier.dtype)
+            if final
+            else jax.ShapeDtypeStruct((tiles, 2 * pixels, COLUMN), jnp.float32),
+            scratch_shapes=[pltpu.VMEM((sum(sizes) * 2 * C, COLUMN), jnp.bfloat16)],
+            compiler_params=params(FOCUS_MIB),
+            cost_estimate=SMALL,
+            name="focus",
+        )(weight, *arrays, total)
+
+    starts = [sum(chunks[:c]) for c in range(len(chunks))]
+    places = [[a * room + starts[c] + i for a in range(4) for i in range(n)] for c, n in enumerate(chunks)]
+    places[0] = [4 * room + i for i in range(2 * cap)] + places[0]
+    weights = [weights_of(p) for p in places]
+    total = earlier.reshape(2 * pixels, width)
+    history = [received]
+    for c in range(len(chunks)):
+        over_x, over_y = history[c]
+        arrays = [over_x, over_y, swap(over_x, 1), swap(over_y, 1)]
+        if c + 1 < len(chunks):
+            coming = (swap(moved[0], 2), swap(moved[1], 4))
+            if c + 2 < len(chunks):
+                begin, n = starts[c + 2], chunks[c + 2]
+                moved = gather(send, flat, halo, [(begin, n, 0), (room + begin, n, 1)], history[: min(c + 1, 2)])
+        total = focus(total, ([own, sibling] if c == 0 else []) + arrays, weights[c], c == len(chunks) - 1)
+        if c + 1 < len(chunks):
+            coming, total, moved, send = lax.optimization_barrier((coming, total, moved, send))
+            history.append(coming)
+    return total.reshape(earlier.shape)
+
+
+def paired_device(echoes, pairing, footprint, counts, offsets, earlier):
+    owners, ranges = lax.axis_size("ping"), lax.axis_size("rng")
+    tiles = footprint.shape[0]
+    ping_dev, _, _, width = echoes.shape
+    cap = -(-MOST // owners)
+    room = 4 * cap
+    base = owners * (owners // 2)
+    flat = echoes.reshape(ping_dev, 2 * C, width)
+    head = lax.slice_in_dim(flat, 0, LANES, axis=2)
+    tail = lax.slice_in_dim(flat, width - LANES, width, axis=2)
+    behind = lax.ppermute(head, "rng", [(i + 1, i) for i in range(ranges - 1)])
+    ahead = lax.ppermute(tail, "rng", [(i, i + 1) for i in range(ranges - 1)])
+    halo = jnp.where(jnp.arange(LANES) < BAND, behind, ahead)
+    last_ping = passed_along(echoes[-1], "ping", 1)
+    me = lax.axis_index("ping").astype(jnp.int32).reshape(1)
+    whole = lambda *shape: jax.ShapeDtypeStruct(shape, jnp.int32)
+    send, masks, shifts, chosen = pl.pallas_call(
+        functools.partial(plan_kernel, owners, ping_dev, cap, tiles),
+        out_shape=[
+            whole(2 * (2 * room + 2 * cap)), whole(base + 2 * owners), whole(tiles * owners * ping_dev), whole(1)
+        ],
+        in_specs=[SMEM] * 4,
+        out_specs=[SMEM] * 4,
+        cost_estimate=SMALL,
+        name="plan",
+    )(footprint, counts, offsets, me)
+    moved = gather(send, flat, halo, [(0, LEAD, 0), (room, LEAD, 1)])
+    received = (swap(moved[0], 2), swap(moved[1], 4))
+    turn = turns(exchanged(after(echoes, moved[0]), pairing, last_ping))
+    later = after(send, moved[0])
+    own, sibling = gather(later, flat, halo, [(2 * room, cap, None), (2 * room + cap, cap, None)])
+    sibling = swap(sibling, 1)
+    coming = gather(after(send, own), flat, halo, [(LEAD, LEAD, 0), (room + LEAD, LEAD, 1)])
+    table = pl.pallas_call(
+        functools.partial(places_kernel, owners, ping_dev, cap),
+        out_shape=whole(3 * (4 * room + 2 * cap)),
+        in_specs=[SMEM] * 6,
+        out_specs=SMEM,
+        cost_estimate=SMALL,
+        name="places",
+    )(footprint, counts, offsets, after(masks, own), shifts, me)
+    return lax.switch(
+        chosen[0],
+        [functools.partial(chunked, v) for v in VARIANTS],
+        counts, me, flat, halo, send, table, turn, coming, received, own, sibling, earlier,
+    )
+
+
+def per_device(echoes, pairing, footprint, counts, offsets, earlier):
+    owners = lax.axis_size("ping")
+    ping_dev = echoes.shape[0]
+    paired = (
+        owners == 8
+        and footprint.shape[0] == owners
+        and ping_dev <= 16
+        and ping_dev & (ping_dev - 1) == 0
+        and sum(VARIANTS[-1]) >= 4 * -(-MOST // owners)
+    )
+    device = paired_device if paired else general_device
+    return device(echoes, pairing, footprint, counts, offsets, earlier)
+
+
 def solution(mesh):
     return jax.shard_map(
         per_device,

time: 450 us -> 184 us (0.41); the launches traced: 443 us -> 182 us
  local copies, waits for them, and re-layouts: 200 us -> 9.86 us
  Pallas kernels: 0 us -> 118 us
  other arithmetic: 79.1 us -> 1.1 us
  waiting for transfers between devices: 75.1 us -> 21.5 us
  matrix products: 41.5 us -> 1.6 us
  blocking collectives: 24.4 us -> 0 us
  starting transfers between devices: 15.5 us -> 28.5 us
  loops' own time: 5.43 us -> 0.36 us
    gather x144 -> x0, local copies, waits for them, and re-layouts: 180 us -> none
    pallas_call x0 -> x15, Pallas kernels: none -> 118 us  [the longest x4 67.4 us: focus(): pl.pallas_call(functools.partial(focus_kernel, sizes), grid=(tiles,), in_...]
    all_to_all x2 -> x0, waiting for transfers between devices: 69 us -> none  [the longest x1 69 us: per_device(): lax.all_to_all(outgoing, 'ping', split_axis=0, concat_axis=0, tiled=True)]
    another operation x6 -> x1, other arithmetic: 67.6 us -> 0.01 us  [exchanged(): parts = jnp.stack([cross_sum, front_energy, rear_energy])]
    dot_general x4 -> x3, matrix products: 41.5 us -> 1.6 us  [the longest x1 0.83 us: exchanged(): jnp.einsum('pkc,pzcr->pzkr', rear_pick, echoes, preferred_element_type=jn...]
    ppermute x2 -> x25, starting transfers between devices: 2.6 us -> 27 us  [the longest x21 16.9 us: swap(): lax.ppermute(shard, 'ping', [(i, i ^ by) for i in range(lax.axis_size('pi...]
    ppermute x2 -> x25, waiting for transfers between devices: 6.09 us -> 21.5 us  [the longest x21 20.2 us: swap(): lax.ppermute(shard, 'ping', [(i, i ^ by) for i in range(lax.axis_size('pi...]
    all_gather x1 -> x0, blocking collectives: 12.4 us -> none  [prefix(): everything = lax.all_gather(shard, axis)]
  transfers between devices with their start and end apart: 5 -> 26, of which waited for: 3 -> 3; matrix products, arithmetic and copies ran while one was open for 64% -> 2% of each run, Pallas kernels for 0% -> 58%
where the time goes in v2:
time: 184 us; the launch traced here: 182 us
  Pallas kernels  118 us (64%)
  starting transfers between devices  28.5 us (15%)
  waiting for transfers between devices  21.5 us (12%)
  local copies, waits for them, and re-layouts  9.86 us (5%)
    pallas_call x4, Pallas kernels, focus(): pl.pallas_call(functools.partial(focus_kernel, sizes), grid=(tiles,), in_...  67.4 us
    pallas_call x4, Pallas kernels, weights_of(): pl.pallas_call(functools.partial(weights_kernel, spacing, pixels), grid=(...  23.9 us
    ppermute x21, waiting for transfers between devices, swap(): lax.ppermute(shard, 'ping', [(i, i ^ by) for i in range(lax.axis_size('pi...  20.2 us
    pallas_call x5, Pallas kernels, gather(): pl.pallas_call(functools.partial(gather_kernel, ping_dev, send.shape[0] /...  20 us
    ppermute x21, starting transfers between devices, swap(): lax.ppermute(shard, 'ping', [(i, i ^ by) for i in range(lax.axis_size('pi...  16.9 us
    cond x8, local copies, waits for them, and re-layouts  6.85 us
    ppermute x1, starting transfers between devices, paired_device(): ahead = lax.ppermute(tail, 'rng', [(i, i + 1) for i in range(ranges - 1)])  5.57 us
    pallas_call x1, Pallas kernels, paired_device(): pl.pallas_call(functools.partial(plan_kernel, owners, ping_dev, cap, tile...  4.43 us
  transfers between devices with their start and end apart: 26, of which 3 were waited for; matrix products, arithmetic and copies ran while one was open for 2% of the time, Pallas kernels for 58%

profile of v2, /device:TPU:0, one launch (start us, length us, event | category | flops | bytes accessed | tf_op | source)
XLA Modules:
  0.0 182.1 jit_solution(7242267087541431866)
XLA Ops:
  0.0 1.1 fusion.16
  1.1 1.3 collective-permute-start.46
  2.4 5.6 %collective-permute-start.47 = (bf16[16,64,128]{2,1,0:T(8,128)(2,1)S(1)}, bf16[16,64,128]{2,1,0:T(8,128)(2,1)S(1)}, u32[]{:S(2)}, u32[]{:S(2)}) collective-permute-start(bf16[16,64,128]{2,1,0:T(8,128)(2,1)S(1)} %get-tuple-element.273), channel_id=1, source_target_pairs={{0,1},{1,2},{2,3},{4,5},{5,6},{6,7},{8,9},{9,10},{10,11},{12,13},{... | collective-permute-start | bytes 786440 | tf_op jit(solution)/shard_map/ppermute | solution.py:688
  8.0 1.0 slice_bitcast_fusion
  8.9 1.5 collective-permute-start.48
  10.4 0.7 slice_bitcast_fusion.4
  11.1 4.4 %plan.1 = (s32[120]{0:T(128)S(1)}, s32[48]{0:T(128)}, s32[1024]{0:T(1024)}, s32[1]{0:T(128)}) custom-call(s32[8,48]{1,0:T(8,128)} %fp.3, s32[8]{0:T(128)} %cnt.3, s32[8,48]{1,0:T(8,128)} %off.3, s32[1]{0:T(128)} %bitcast.6.me_ref), custom_call_target="tpu_custom_call" | custom-call | flops 1024 | bytes 1024 | tf_op jit(solution)/shard_map/plan/pallas_call | solution.py:693
  15.9 4.7 %gather.17 = (bf16[4,64,2048]{2,1,0:T(8,128)(2,1)}, bf16[4,64,2048]{2,1,0:T(8,128)(2,1)S(1)}) custom-call(s32[120]{0:T(128)S(1)} %get-tuple-element.259.send, bf16[16,64,2048]{2,1,0:T(8,128)(2,1)} %bitcast.46, bf16[16,64,128]{2,1,0:T(8,128)(2,1)S(1)} %broadcast_select_fusion.halo), custom_call_target="tpu_custom_call" | custom-call | flops 1024 | bytes 1024 | tf_op jit(solution)/shard_map/gather/pallas_call | solution.py:599
  20.6 0.6 convolution_bitcast_fusion.1
  21.3 0.8 multiply_reduce_fusion
  22.2 0.3 fusion.1
  22.5 0.3 fusion.5
  22.9 1.9 %collective-permute-start.49 = (f32[3,16]{1,0:T(4,128)S(1)}, f32[3,16]{1,0:T(4,128)S(1)}, u32[]{:S(2)}, u32[]{:S(2)}) collective-permute-start(f32[3,16]{1,0:T(4,128)S(1)} %pad_maximum_fusion.1), channel_id=1, source_target_pairs={{0,1},{1,0},{2,3},{3,2},{4,5},{5,4},{6,7},{7,6},{8,9},{9,8},{10,11... | collective-permute-start | bytes 584 | tf_op jit(solution)/shard_map/ppermute | solution.py:579
  24.8 4.1 %gather.18 = (bf16[6,64,2048]{2,1,0:T(8,128)(2,1)}, bf16[6,64,2048]{2,1,0:T(8,128)(2,1)S(1)}) custom-call(s32[120]{0:T(128)S(1)} %get-tuple-element.259.send, bf16[16,64,2048]{2,1,0:T(8,128)(2,1)S(1)} %bitcast.50, bf16[16,64,128]{2,1,0:T(8,128)(2,1)S(1)} %broadcast_select_fusion.halo), custom_call_target="tpu_custom_call" | custom-call | flops 1024 | bytes 1024 | tf_op jit(solution)/shard_map/gather/pallas_call | solution.py:599
  28.9 1.9 %collective-permute-start.57 = (bf16[6,64,2048]{2,1,0:T(8,128)(2,1)S(1)}, bf16[6,64,2048]{2,1,0:T(8,128)(2,1)}, u32[]{:S(2)}, u32[]{:S(2)}) collective-permute-start(bf16[6,64,2048]{2,1,0:T(8,128)(2,1)S(1)} %get-tuple-element.263), channel_id=1, source_target_pairs={{0,4},{4,0},{8,12},{12,8},{16,20},{20,16},{24,28},{28,24},{1,5},{5... | collective-permute-start | bytes 4718600 | tf_op jit(solution)/shard_map/ppermute | solution.py:548
  30.9 1.4 collective-permute-start.50
  32.3 1.9 %collective-permute-start.55 = (bf16[4,64,2048]{2,1,0:T(8,128)(2,1)}, bf16[4,64,2048]{2,1,0:T(8,128)(2,1)}, u32[]{:S(2)}, u32[]{:S(2)}) collective-permute-start(bf16[4,64,2048]{2,1,0:T(8,128)(2,1)} %get-tuple-element.253), channel_id=1, source_target_pairs={{0,8},{4,12},{8,0},{12,4},{16,24},{20,28},{24,16},{28,20},{1,9},{5... | collective-permute-start | bytes 3145736 | tf_op jit(solution)/shard_map/ppermute | solution.py:548
  34.2 1.2 collective-permute-done.50
  35.5 1.2 collective-permute-done.51
  36.8 1.9 %collective-permute-start.52 = (f32[3,8,16]{2,1,0:T(8,128)S(1)}, f32[3,8,16]{2,1,0:T(8,128)S(1)}, u32[]{:S(2)}, u32[]{:S(2)}) collective-permute-start(f32[3,8,16]{2,1,0:T(8,128)S(1)} %fusion.14), channel_id=1, source_target_pairs={{0,8},{4,12},{8,0},{12,4},{16,24},{20,28},{24,16},{28,20},{1,9},{5... | collective-permute-start | bytes 4616 | tf_op jit(solution)/shard_map/ppermute | solution.py:548
  38.7 19.0 %collective-permute-done.52 = f32[3,8,16]{2,1,0:T(8,128)S(1)} collective-permute-done((f32[3,8,16]{2,1,0:T(8,128)S(1)}, f32[3,8,16]{2,1,0:T(8,128)S(1)}, u32[]{:S(2)}, u32[]{:S(2)}) %collective-permute-start.52) | collective-permute-done | bytes 1568 | tf_op jit(solution)/shard_map/ppermute | solution.py:548
  57.8 1.2 collective-permute-start.54
  59.5 3.5 %gather.19 = (bf16[4,64,2048]{2,1,0:T(8,128)(2,1)}, bf16[4,64,2048]{2,1,0:T(8,128)(2,1)}) custom-call(s32[120]{0:T(128)S(1)} %get-tuple-element.259.send, bf16[16,64,2048]{2,1,0:T(8,128)(2,1)S(1)} %bitcast.51, bf16[16,64,128]{2,1,0:T(8,128)(2,1)S(1)} %broadcast_select_fusion.halo), custom_call_target="tpu_custom_call" | custom-call | flops 1024 | bytes 1024 | tf_op jit(solution)/shard_map/gather/pallas_call | solution.py:599
  63.0 2.6 %places.1 = s32[324]{0:T(512)S(1)} custom-call(s32[8,48]{1,0:T(8,128)} %fp.3, s32[8]{0:T(128)S(1)} %copy-done.14, s32[8,48]{1,0:T(8,128)} %off.3, s32[48]{0:T(128)} %get-tuple-element.256.masks, s32[1024]{0:T(1024)} %get-tuple-element.257.shifts, s32[1]{0:T(128)} %bitcast.6.me_ref), custom_call_target="tpu_custom_call" | custom-call | flops 1024 | bytes 1024 | tf_op jit(solution)/shard_map/places/pallas_call | solution.py:710
  66.1 116.0 %conditional.1 = (bf16[1,2,1024,2048]{3,2,1,0:T(8,128)(2,1)}) conditional(s32[]{:T(128)} %bitcast.7, (s32[324]{0:T(512)S(1)}, s32[16]{0:T(128)S(1)}, s32[8]{0:T(128)S(1)}, s32[1]{0:T(128)}, f32[128]{0:T(128)S(1)}, /*index=5*/bf16[4,64,2048]{2,1,0:T(8,128)(2,1)}, bf16[4,64,2048]{2,1,0:T(8,128)(2,1)}, s32[28]{0:T(128)S(1)}, ...), branch_computations={%region_4.5_spmd, %region_5.6_spmd, %region_6.7_spmd} | conditional | flops 16384 | bytes 205538304 | solution.py:718
  66.4 0.5 collective-permute-start.13
  66.9 2.3 %collective-permute-start.10 = (bf16[4,64,2048]{2,1,0:T(8,128)(2,1)}, bf16[4,64,2048]{2,1,0:T(8,128)(2,1)S(1)}, u32[]{:S(2)}, u32[]{:S(2)}) collective-permute-start(bf16[4,64,2048]{2,1,0:T(8,128)(2,1)} %get-tuple-element.151), channel_id=1, source_target_pairs={{0,8},{4,12},{8,0},{12,4},{16,24},{20,28},{24,16},{28,20},{1,9},{5... | collective-permute-start | bytes 3145736 | tf_op jit(solution)/shard_map/cond/branch_1_fun/ppermute | solution.py:548
  69.3 4.3 %gather.11 = (bf16[4,64,2048]{2,1,0:T(8,128)(2,1)}, bf16[4,64,2048]{2,1,0:T(8,128)(2,1)}) custom-call(s32[120]{0:T(128)S(1)} %get-tuple-element.170.send, bf16[16,64,2048]{2,1,0:T(8,128)(2,1)} %get-tuple-element.160.echoes, bf16[16,64,128]{2,1,0:T(8,128)(2,1)S(1)} %get-tuple-element.161.halo, bf16[4,64,2048]{2,1,0:T(8,128)(2,1)} %get-tuple-element.156.refs_2_.refs_0_, ...), custom_call_target="tpu_custom_call" | custom-call | flops 1024 | bytes 1024 | tf_op jit(solution)/shard_map/cond/branch_1_fun/gather/pallas_call | solution.py:599
  73.5 8.4 %weights.17 = bf16[2048,1792]{1,0:T(8,128)(2,1)} custom-call(s32[324]{0:T(512)S(1)} %get-tuple-element.146.table, s32[28]{0:T(128)S(1)} %get-tuple-element.153.where, s32[8]{0:T(128)S(1)} %get-tuple-element.148.cnt, s32[1]{0:T(128)} %get-tuple-element.149.me_ref, f32[128]{0:T(128)S(1)} %get-tuple-element.150.turn_ref), custom_call_target="tpu_custom_call" | custom-call | flops 1024 | bytes 1024 | tf_op jit(solution)/shard_map/cond/branch_1_fun/weights/pallas_call | solution.py:625
  82.0 3.1 %copy-done.1 = bf16[2048,1792]{1,0:T(8,128)(2,1)S(1)} copy-done((bf16[2048,1792]{1,0:T(8,128)(2,1)S(1)}, bf16[2048,1792]{1,0:T(8,128)(2,1)}, u32[]{:S(2)}) %copy-start.1) | copy-done | bytes 7340056 | tf_op jit(solution)/shard_map/cond
  85.0 22.5 %focus.16.refs_4_ = f32[4,2048,512]{2,1,0:T(8,128)} custom-call(bf16[2048,1792]{1,0:T(8,128)(2,1)S(1)} %copy-done.1, bf16[6,64,2048]{2,1,0:T(8,128)(2,1)} %get-tuple-element.154.refs_0_, bf16[6,64,2048]{2,1,0:T(8,128)(2,1)} %get-tuple-element.155.refs_1_, bf16[4,64,2048]{2,1,0:T(8,128)(2,1)} %get-tuple-element.156.refs_2_.refs_0_, ...), custom_call_target="tpu_custom_call" | custom-call | flops 1024 | bytes 1024 | tf_op jit(solution)/shard_map/cond/branch_1_fun/focus/pallas_call | solution.py:642
  107.5 0.2 collective-permute-start.16
  107.7 0.4 collective-permute-start.17
  108.1 2.8 %collective-permute-start.14 = (bf16[4,64,2048]{2,1,0:T(8,128)(2,1)}, bf16[4,64,2048]{2,1,0:T(8,128)(2,1)S(1)}, u32[]{:S(2)}, u32[]{:S(2)}) collective-permute-start(bf16[4,64,2048]{2,1,0:T(8,128)(2,1)} %get-tuple-element.164), channel_id=1, source_target_pairs={{0,8},{4,12},{8,0},{12,4},{16,24},{20,28},{24,16},{28,20},{1,9},{5... | collective-permute-start | bytes 3145736 | tf_op jit(solution)/shard_map/cond/branch_1_fun/ppermute | solution.py:548
  110.9 5.7 %weights.18 = bf16[2048,1024]{1,0:T(8,128)(2,1)} custom-call(s32[324]{0:T(512)S(1)} %get-tuple-element.146.table, s32[16]{0:T(128)S(1)} %get-tuple-element.166.where, s32[8]{0:T(128)S(1)} %get-tuple-element.148.cnt, s32[1]{0:T(128)} %get-tuple-element.149.me_ref, f32[128]{0:T(128)S(1)} %get-tuple-element.150.turn_ref), custom_call_target="tpu_custom_call" | custom-call | flops 1024 | bytes 1024 | tf_op jit(solution)/shard_map/cond/branch_1_fun/weights/pallas_call | solution.py:625
  116.6 3.4 %gather.12 = (bf16[2,64,2048]{2,1,0:T(8,128)(2,1)}, bf16[2,64,2048]{2,1,0:T(8,128)(2,1)}) custom-call(s32[120]{0:T(128)S(1)} %get-tuple-element.170.send, bf16[16,64,2048]{2,1,0:T(8,128)(2,1)} %get-tuple-element.160.echoes, bf16[16,64,128]{2,1,0:T(8,128)(2,1)S(1)} %get-tuple-element.161.halo, bf16[4,64,2048]{2,1,0:T(8,128)(2,1)} %get-tuple-element.156.refs_2_.refs_0_, ...), custom_call_target="tpu_custom_call" | custom-call | flops 1024 | bytes 1024 | tf_op jit(solution)/shard_map/cond/branch_1_fun/gather/pallas_call | solution.py:599
  120.0 16.7 %focus.17.refs_4_ = f32[4,2048,512]{2,1,0:T(8,128)} custom-call(bf16[2048,1024]{1,0:T(8,128)(2,1)S(1)} %copy-done.4, bf16[4,64,2048]{2,1,0:T(8,128)(2,1)S(1)} %collective-permute-done.10.refs_0_.refs_2_, bf16[4,64,2048]{2,1,0:T(8,128)(2,1)S(1)} %collective-permute-done.11.refs_1_.refs_3_, bf16[4,64,2048]{2,1,0:T(8,128)(2,1)} %collective-permute-done.16.refs_2_, ...), custom_call_target="tpu_custom_call" | custom-call | flops 1024 | bytes 1024 | tf_op jit(solution)/shard_map/cond/branch_1_fun/focus/pallas_call | solution.py:642
  136.7 0.3 collective-permute-start.20
  137.0 0.3 collective-permute-start.21
  137.3 1.7 collective-permute-start.18
  139.0 0.7 collective-permute-start.19
  139.7 5.7 %weights.19 = bf16[2048,1024]{1,0:T(8,128)(2,1)} custom-call(s32[324]{0:T(512)S(1)} %get-tuple-element.146.table, s32[16]{0:T(128)S(1)} %get-tuple-element.175.where, s32[8]{0:T(128)S(1)} %get-tuple-element.148.cnt, s32[1]{0:T(128)} %get-tuple-element.149.me_ref, f32[128]{0:T(128)S(1)} %get-tuple-element.150.turn_ref), custom_call_target="tpu_custom_call" | custom-call | flops 1024 | bytes 1024 | tf_op jit(solution)/shard_map/cond/branch_1_fun/weights/pallas_call | solution.py:625
  145.4 2.2 %copy-done.9 = bf16[2048,1024]{1,0:T(8,128)(2,1)S(1)} copy-done((bf16[2048,1024]{1,0:T(8,128)(2,1)S(1)}, bf16[2048,1024]{1,0:T(8,128)(2,1)}, u32[]{:S(2)}) %copy-start.9) | copy-done | bytes 4194328 | tf_op jit(solution)/shard_map/cond
  147.6 16.3 %focus.18.refs_4_ = f32[4,2048,512]{2,1,0:T(8,128)} custom-call(bf16[2048,1024]{1,0:T(8,128)(2,1)S(1)} %copy-done.9, bf16[4,64,2048]{2,1,0:T(8,128)(2,1)S(1)} %collective-permute-done.14.refs_0_, bf16[4,64,2048]{2,1,0:T(8,128)(2,1)} %collective-permute-done.15.refs_1_, bf16[4,64,2048]{2,1,0:T(8,128)(2,1)S(1)} %collective-permute-done.20.refs_2_, ...), custom_call_target="tpu_custom_call" | custom-call | flops 1024 | bytes 1024 | tf_op jit(solution)/shard_map/cond/branch_1_fun/focus/pallas_call | solution.py:642
  164.0 0.5 collective-permute-start.23
  164.5 4.1 %weights.16 = bf16[2048,512]{1,0:T(8,128)(2,1)} custom-call(s32[324]{0:T(512)S(1)} %get-tuple-element.146.table, s32[8]{0:T(128)} %constant.39.clone.1.where, s32[8]{0:T(128)S(1)} %get-tuple-element.148.cnt, s32[1]{0:T(128)} %get-tuple-element.149.me_ref, f32[128]{0:T(128)S(1)} %get-tuple-element.150.turn_ref), custom_call_target="tpu_custom_call" | custom-call | flops 1024 | bytes 1024 | tf_op jit(solution)/shard_map/cond/branch_1_fun/weights/pallas_call | solution.py:625
  168.6 1.6 copy-done.12
  170.2 11.9 %focus.19 = bf16[2048,2048]{1,0:T(8,128)(2,1)} custom-call(bf16[2048,512]{1,0:T(8,128)(2,1)S(1)} %copy-done.12, bf16[2,64,2048]{2,1,0:T(8,128)(2,1)} %collective-permute-done.18.refs_0_, bf16[2,64,2048]{2,1,0:T(8,128)(2,1)} %collective-permute-done.19.refs_1_, bf16[2,64,2048]{2,1,0:T(8,128)(2,1)S(1)} %collective-permute-done.22.refs_2_, ...), custom_call_target="tpu_custom_call" | custom-call | flops 1024 | bytes 1024 | tf_op jit(solution)/shard_map/cond/branch_1_fun/focus/pallas_call | solution.py:642
  (62 shorter events, 1.2 us)
Async XLA Ops:
  1.1 14.7 %collective-permute-start.46 = (bf16[16,64,128]{2,1,0:T(8,128)(2,1)S(1)}, bf16[16,64,128]{2,1,0:T(8,128)(2,1)S(1)}, u32[]{:S(2)}, u32[]{:S(2)}) collective-permute-start(bf16[16,64,128]{2,1,0:T(8,128)(2,1)S(1)} %get-tuple-element.274), channel_id=1, source_target_pairs={{1,0},{2,1},{3,2},{5,4},{6,5},{7,6},{9,8},{10,9},{11,10},{13,12},{... | collective-permute-start | bytes 786440 | tf_op jit(solution)/shard_map/ppermute | solution.py:687
  2.4 13.5 %collective-permute-start.47 = (bf16[16,64,128]{2,1,0:T(8,128)(2,1)S(1)}, bf16[16,64,128]{2,1,0:T(8,128)(2,1)S(1)}, u32[]{:S(2)}, u32[]{:S(2)}) collective-permute-start(bf16[16,64,128]{2,1,0:T(8,128)(2,1)S(1)} %get-tuple-element.273), channel_id=1, source_target_pairs={{0,1},{1,2},{2,3},{4,5},{5,6},{6,7},{8,9},{9,10},{10,11},{12,13},{... | collective-permute-start | bytes 786440 | tf_op jit(solution)/shard_map/ppermute | solution.py:688
  8.9 13.2 %collective-permute-start.48 = (bf16[2,32,2048]{2,1,0:T(8,128)(2,1)S(1)}, bf16[2,32,2048]{2,1,0:T(8,128)(2,1)S(1)}, u32[]{:S(2)}, u32[]{:S(2)}) collective-permute-start(bf16[2,32,2048]{2,1,0:T(8,128)(2,1)S(1)} %slice_bitcast_fusion), channel_id=1, source_target_pairs={{0,4},{4,8},{8,12},{12,16},{16,20},{20,24},{24,28},{1,5},{5,9},{9,... | collective-permute-start | bytes 786440 | tf_op jit(solution)/shard_map/ppermute | solution.py:27
  15.7 4.9 %copy-start.13 = (bf16[16,2,32,2048]{3,2,1,0:T(8,128)(2,1)S(1)}, bf16[16,2,32,2048]{3,2,1,0:T(8,128)(2,1)}, u32[]{:S(2)}) copy-start(bf16[16,2,32,2048]{3,2,1,0:T(8,128)(2,1)} %param.22) | copy-start | bytes 12582916
  22.8 40.2 %copy-start.14 = (s32[8]{0:T(128)S(1)}, s32[8]{0:T(128)}, u32[]{:S(2)}) copy-start(s32[8]{0:T(128)} %cnt.3) | copy-start | bytes 100
  22.8 43.2 %copy-start.15 = (s32[28]{0:T(128)S(1)}, s32[28]{0:T(128)}, u32[]{:S(2)}) copy-start(s32[28]{0:T(128)} %constant.36.clone) | copy-start | bytes 340
  22.8 43.2 %copy-start.16 = (s32[16]{0:T(128)S(1)}, s32[16]{0:T(128)}, u32[]{:S(2)}) copy-start(s32[16]{0:T(128)} %constant.37.clone) | copy-start | bytes 196
  22.9 43.2 %copy-start.17 = (s32[16]{0:T(128)S(1)}, s32[16]{0:T(128)}, u32[]{:S(2)}) copy-start(s32[16]{0:T(128)} %constant.38.clone) | copy-start | bytes 196
  22.9 8.0 %collective-permute-start.49 = (f32[3,16]{1,0:T(4,128)S(1)}, f32[3,16]{1,0:T(4,128)S(1)}, u32[]{:S(2)}, u32[]{:S(2)}) collective-permute-start(f32[3,16]{1,0:T(4,128)S(1)} %pad_maximum_fusion.1), channel_id=1, source_target_pairs={{0,1},{1,0},{2,3},{3,2},{4,5},{5,4},{6,7},{7,6},{8,9},{9,8},{10,11... | collective-permute-start | bytes 584 | tf_op jit(solution)/shard_map/ppermute | solution.py:579
  28.9 37.1 %collective-permute-start.57 = (bf16[6,64,2048]{2,1,0:T(8,128)(2,1)S(1)}, bf16[6,64,2048]{2,1,0:T(8,128)(2,1)}, u32[]{:S(2)}, u32[]{:S(2)}) collective-permute-start(bf16[6,64,2048]{2,1,0:T(8,128)(2,1)S(1)} %get-tuple-element.263), channel_id=1, source_target_pairs={{0,4},{4,0},{8,12},{12,8},{16,20},{20,16},{24,28},{28,24},{1,5},{5... | collective-permute-start | bytes 4718600 | tf_op jit(solution)/shard_map/ppermute | solution.py:548
  30.9 4.5 %collective-permute-start.50 = (f32[3,16]{1,0:T(4,128)S(1)}, f32[3,16]{1,0:T(4,128)S(1)}, u32[]{:S(2)}, u32[]{:S(2)}) collective-permute-start(f32[3,16]{1,0:T(4,128)S(1)} %fusion.15), channel_id=1, source_target_pairs={{0,2},{1,3},{2,0},{3,1},{4,6},{5,7},{6,4},{7,5},{8,10},{9,11},{10,... | collective-permute-start | bytes 584 | tf_op jit(solution)/shard_map/ppermute | solution.py:579
  32.3 33.8 %collective-permute-start.55 = (bf16[4,64,2048]{2,1,0:T(8,128)(2,1)}, bf16[4,64,2048]{2,1,0:T(8,128)(2,1)}, u32[]{:S(2)}, u32[]{:S(2)}) collective-permute-start(bf16[4,64,2048]{2,1,0:T(8,128)(2,1)} %get-tuple-element.253), channel_id=1, source_target_pairs={{0,8},{4,12},{8,0},{12,4},{16,24},{20,28},{24,16},{28,20},{1,9},{5... | collective-permute-start | bytes 3145736 | tf_op jit(solution)/shard_map/ppermute | solution.py:548
  34.2 31.8 %collective-permute-start.56 = (bf16[4,64,2048]{2,1,0:T(8,128)(2,1)S(1)}, bf16[4,64,2048]{2,1,0:T(8,128)(2,1)}, u32[]{:S(2)}, u32[]{:S(2)}) collective-permute-start(bf16[4,64,2048]{2,1,0:T(8,128)(2,1)S(1)} %get-tuple-element.262), channel_id=1, source_target_pairs={{0,16},{4,20},{8,24},{12,28},{16,0},{20,4},{24,8},{28,12},{1,17},{... | collective-permute-start | bytes 3145736 | tf_op jit(solution)/shard_map/ppermute | solution.py:548
  35.5 1.2 collective-permute-start.51
  36.8 21.0 %collective-permute-start.52 = (f32[3,8,16]{2,1,0:T(8,128)S(1)}, f32[3,8,16]{2,1,0:T(8,128)S(1)}, u32[]{:S(2)}, u32[]{:S(2)}) collective-permute-start(f32[3,8,16]{2,1,0:T(8,128)S(1)} %fusion.14), channel_id=1, source_target_pairs={{0,8},{4,12},{8,0},{12,4},{16,24},{20,28},{24,16},{28,20},{1,9},{5... | collective-permute-start | bytes 4616 | tf_op jit(solution)/shard_map/ppermute | solution.py:548
  38.7 27.0 %collective-permute-start.53 = (f32[3,8,16]{2,1,0:T(8,128)S(1)}, f32[3,8,16]{2,1,0:T(8,128)S(1)}, u32[]{:S(2)}, u32[]{:S(2)}) collective-permute-start(f32[3,8,16]{2,1,0:T(8,128)S(1)} %fusion.14), channel_id=1, source_target_pairs={{0,16},{4,20},{8,24},{12,28},{16,0},{20,4},{24,8},{28,12},{1,17},{... | collective-permute-start | bytes 4616 | tf_op jit(solution)/shard_map/ppermute | solution.py:548
  57.8 8.0 %collective-permute-start.54 = (f32[3,8,16]{2,1,0:T(8,128)S(1)}, f32[3,8,16]{2,1,0:T(8,128)S(1)}, u32[]{:S(2)}, u32[]{:S(2)}) collective-permute-start(f32[3,8,16]{2,1,0:T(8,128)S(1)} %fusion.14), channel_id=1, source_target_pairs={{0,24},{4,28},{8,16},{12,20},{16,8},{20,12},{24,0},{28,4},{1,25},{... | collective-permute-start | bytes 4616 | tf_op jit(solution)/shard_map/ppermute | solution.py:548
  66.3 15.6 %collective-permute-start.12 = (bf16[4,64,2048]{2,1,0:T(8,128)(2,1)}, bf16[4,64,2048]{2,1,0:T(8,128)(2,1)S(1)}, u32[]{:S(2)}, u32[]{:S(2)}) collective-permute-start(bf16[4,64,2048]{2,1,0:T(8,128)(2,1)} %get-tuple-element.156.refs_2_.refs_0_), channel_id=1, source_target_pairs={{0,4},{4,0},{8,12},{12,8},{16,20},{20,16},{24,28},{28,24},{1,5},{5... | collective-permute-start | bytes 3145736 | tf_op jit(solution)/shard_map/cond/branch_1_fun/ppermute | solution.py:548
  66.4 15.5 %collective-permute-start.13 = (bf16[4,64,2048]{2,1,0:T(8,128)(2,1)}, bf16[4,64,2048]{2,1,0:T(8,128)(2,1)}, u32[]{:S(2)}, u32[]{:S(2)}) collective-permute-start(bf16[4,64,2048]{2,1,0:T(8,128)(2,1)} %get-tuple-element.157.refs_3_.refs_1_), channel_id=1, source_target_pairs={{0,4},{4,0},{8,12},{12,8},{16,20},{20,16},{24,28},{28,24},{1,5},{5... | collective-permute-start | bytes 3145736 | tf_op jit(solution)/shard_map/cond/branch_1_fun/ppermute | solution.py:548
  66.9 40.6 %collective-permute-start.10 = (bf16[4,64,2048]{2,1,0:T(8,128)(2,1)}, bf16[4,64,2048]{2,1,0:T(8,128)(2,1)S(1)}, u32[]{:S(2)}, u32[]{:S(2)}) collective-permute-start(bf16[4,64,2048]{2,1,0:T(8,128)(2,1)} %get-tuple-element.151), channel_id=1, source_target_pairs={{0,8},{4,12},{8,0},{12,4},{16,24},{20,28},{24,16},{28,20},{1,9},{5... | collective-permute-start | bytes 3145736 | tf_op jit(solution)/shard_map/cond/branch_1_fun/ppermute | solution.py:548
  69.2 38.3 %collective-permute-start.11 = (bf16[4,64,2048]{2,1,0:T(8,128)(2,1)}, bf16[4,64,2048]{2,1,0:T(8,128)(2,1)S(1)}, u32[]{:S(2)}, u32[]{:S(2)}) collective-permute-start(bf16[4,64,2048]{2,1,0:T(8,128)(2,1)} %get-tuple-element.152), channel_id=1, source_target_pairs={{0,16},{4,20},{8,24},{12,28},{16,0},{20,4},{24,8},{28,12},{1,17},{... | collective-permute-start | bytes 3145736 | tf_op jit(solution)/shard_map/cond/branch_1_fun/ppermute | solution.py:548
  82.0 3.1 %copy-start.1 = (bf16[2048,1792]{1,0:T(8,128)(2,1)S(1)}, bf16[2048,1792]{1,0:T(8,128)(2,1)}, u32[]{:S(2)}) copy-start(bf16[2048,1792]{1,0:T(8,128)(2,1)} %weights.17) | copy-start | bytes 22020100 | tf_op jit(solution)/shard_map/cond
  107.5 12.5 %collective-permute-start.16 = (bf16[4,64,2048]{2,1,0:T(8,128)(2,1)S(1)}, bf16[4,64,2048]{2,1,0:T(8,128)(2,1)}, u32[]{:S(2)}, u32[]{:S(2)}) collective-permute-start(bf16[4,64,2048]{2,1,0:T(8,128)(2,1)S(1)} %collective-permute-done.10.refs_0_.refs_2_), channel_id=1, source_target_pairs={{0,4},{4,0},{8,12},{12,8},{16,20},{20,16},{24,28},{28,24},{1,5},{5... | collective-permute-start | bytes 3145736 | tf_op jit(solution)/shard_map/cond/branch_1_fun/ppermute | solution.py:548
  107.7 12.3 %collective-permute-start.17 = (bf16[4,64,2048]{2,1,0:T(8,128)(2,1)S(1)}, bf16[4,64,2048]{2,1,0:T(8,128)(2,1)}, u32[]{:S(2)}, u32[]{:S(2)}) collective-permute-start(bf16[4,64,2048]{2,1,0:T(8,128)(2,1)S(1)} %collective-permute-done.11.refs_1_.refs_3_), channel_id=1, source_target_pairs={{0,4},{4,0},{8,12},{12,8},{16,20},{20,16},{24,28},{28,24},{1,5},{5... | collective-permute-start | bytes 3145736 | tf_op jit(solution)/shard_map/cond/branch_1_fun/ppermute | solution.py:548
  108.1 28.6 %collective-permute-start.14 = (bf16[4,64,2048]{2,1,0:T(8,128)(2,1)}, bf16[4,64,2048]{2,1,0:T(8,128)(2,1)S(1)}, u32[]{:S(2)}, u32[]{:S(2)}) collective-permute-start(bf16[4,64,2048]{2,1,0:T(8,128)(2,1)} %get-tuple-element.164), channel_id=1, source_target_pairs={{0,8},{4,12},{8,0},{12,4},{16,24},{20,28},{24,16},{28,20},{1,9},{5... | collective-permute-start | bytes 3145736 | tf_op jit(solution)/shard_map/cond/branch_1_fun/ppermute | solution.py:548
  110.9 25.8 %collective-permute-start.15 = (bf16[4,64,2048]{2,1,0:T(8,128)(2,1)}, bf16[4,64,2048]{2,1,0:T(8,128)(2,1)}, u32[]{:S(2)}, u32[]{:S(2)}) collective-permute-start(bf16[4,64,2048]{2,1,0:T(8,128)(2,1)} %get-tuple-element.165), channel_id=1, source_target_pairs={{0,16},{4,20},{8,24},{12,28},{16,0},{20,4},{24,8},{28,12},{1,17},{... | collective-permute-start | bytes 3145736 | tf_op jit(solution)/shard_map/cond/branch_1_fun/ppermute | solution.py:548
  116.6 3.4 %copy-start.4 = (bf16[2048,1024]{1,0:T(8,128)(2,1)S(1)}, bf16[2048,1024]{1,0:T(8,128)(2,1)}, u32[]{:S(2)}) copy-start(bf16[2048,1024]{1,0:T(8,128)(2,1)} %weights.18) | copy-start | bytes 12582916 | tf_op jit(solution)/shard_map/cond
  136.7 8.7 %collective-permute-start.20 = (bf16[4,64,2048]{2,1,0:T(8,128)(2,1)S(1)}, bf16[4,64,2048]{2,1,0:T(8,128)(2,1)S(1)}, u32[]{:S(2)}, u32[]{:S(2)}) collective-permute-start(bf16[4,64,2048]{2,1,0:T(8,128)(2,1)S(1)} %collective-permute-done.14.refs_0_), channel_id=1, source_target_pairs={{0,4},{4,0},{8,12},{12,8},{16,20},{20,16},{24,28},{28,24},{1,5},{5... | collective-permute-start | bytes 3145736 | tf_op jit(solution)/shard_map/cond/branch_1_fun/ppermute | solution.py:548
  137.0 8.4 %collective-permute-start.21 = (bf16[4,64,2048]{2,1,0:T(8,128)(2,1)}, bf16[4,64,2048]{2,1,0:T(8,128)(2,1)S(1)}, u32[]{:S(2)}, u32[]{:S(2)}) collective-permute-start(bf16[4,64,2048]{2,1,0:T(8,128)(2,1)} %collective-permute-done.15.refs_1_), channel_id=1, source_target_pairs={{0,4},{4,0},{8,12},{12,8},{16,20},{20,16},{24,28},{28,24},{1,5},{5... | collective-permute-start | bytes 3145736 | tf_op jit(solution)/shard_map/cond/branch_1_fun/ppermute | solution.py:548
  137.3 26.7 %collective-permute-start.18 = (bf16[2,64,2048]{2,1,0:T(8,128)(2,1)}, bf16[2,64,2048]{2,1,0:T(8,128)(2,1)}, u32[]{:S(2)}, u32[]{:S(2)}) collective-permute-start(bf16[2,64,2048]{2,1,0:T(8,128)(2,1)} %get-tuple-element.173), channel_id=1, source_target_pairs={{0,8},{4,12},{8,0},{12,4},{16,24},{20,28},{24,16},{28,20},{1,9},{5... | collective-permute-start | bytes 1572872 | tf_op jit(solution)/shard_map/cond/branch_1_fun/ppermute | solution.py:548
  139.0 25.0 %collective-permute-start.19 = (bf16[2,64,2048]{2,1,0:T(8,128)(2,1)}, bf16[2,64,2048]{2,1,0:T(8,128)(2,1)}, u32[]{:S(2)}, u32[]{:S(2)}) collective-permute-start(bf16[2,64,2048]{2,1,0:T(8,128)(2,1)} %get-tuple-element.174), channel_id=1, source_target_pairs={{0,16},{4,20},{8,24},{12,28},{16,0},{20,4},{24,8},{28,12},{1,17},{... | collective-permute-start | bytes 1572872 | tf_op jit(solution)/shard_map/cond/branch_1_fun/ppermute | solution.py:548
  145.4 2.2 %copy-start.9 = (bf16[2048,1024]{1,0:T(8,128)(2,1)S(1)}, bf16[2048,1024]{1,0:T(8,128)(2,1)}, u32[]{:S(2)}) copy-start(bf16[2048,1024]{1,0:T(8,128)(2,1)} %weights.19) | copy-start | bytes 12582916 | tf_op jit(solution)/shard_map/cond
  164.0 4.7 %collective-permute-start.22 = (bf16[2,64,2048]{2,1,0:T(8,128)(2,1)}, bf16[2,64,2048]{2,1,0:T(8,128)(2,1)S(1)}, u32[]{:S(2)}, u32[]{:S(2)}) collective-permute-start(bf16[2,64,2048]{2,1,0:T(8,128)(2,1)} %collective-permute-done.18.refs_0_), channel_id=1, source_target_pairs={{0,4},{4,0},{8,12},{12,8},{16,20},{20,16},{24,28},{28,24},{1,5},{5... | collective-permute-start | bytes 1572872 | tf_op jit(solution)/shard_map/cond/branch_1_fun/ppermute | solution.py:548
  164.0 4.6 %collective-permute-start.23 = (bf16[2,64,2048]{2,1,0:T(8,128)(2,1)}, bf16[2,64,2048]{2,1,0:T(8,128)(2,1)S(1)}, u32[]{:S(2)}, u32[]{:S(2)}) collective-permute-start(bf16[2,64,2048]{2,1,0:T(8,128)(2,1)} %collective-permute-done.19.refs_1_), channel_id=1, source_target_pairs={{0,4},{4,0},{8,12},{12,8},{16,20},{20,16},{24,28},{28,24},{1,5},{5... | collective-permute-start | bytes 1572872 | tf_op jit(solution)/shard_map/cond/branch_1_fun/ppermute | solution.py:548
  168.6 1.6 copy-start.12
